TPU v7x, 128 devices: a whole 4x4x4 slice. The times are simulated.
128 devices in a mesh: row: 32 (over z, y, core), ctr: 4 (over x).
Axes of the slice: x: 4, y: 4, z: 4, core: 2. Of those that a mesh axis runs over, the one named last changes fastest.
Arguments:
- embeddings: bfloat16 [98304, 1536], P(('row', 'ctr')), may hold values from -7 to 7
- centroids: bfloat16 [512, 256, 1536], P('row', 'ctr'), may hold values from -6 to 6
- candidates: int32 [128, 6], P(('row', 'ctr')), may hold values from 0 to 511, as said below
Outputs:
- new_centroids: bfloat16 [512, 256, 1536], P('row', 'ctr')
- nearest: float32 [98304], P(('row', 'ctr'))
Inputs may be any that keep to these rules, and one draw needn't show every extreme that they name: `candidates`: block b is owned by index b // 16 of row. Each row names 6 blocks of 6 different owners. The 4 row blocks of one index of row name at most one block of each owner (the same block wherever that owner appears).
All inputs are finite; a program needn't handle non-finite values.
Results may differ from a plain program's by a relative error of at most 0.007.
Values may be sent and summed in bfloat16 or wider, within the bound.
A program may use at most 128 MiB of HBM per device.

v0:
```python
import math

import jax
import jax.numpy as jnp
from jax import lax
from jax.sharding import PartitionSpec as P

score_scale = 1.5
epsilon = 1e-06


def on_device(embeddings, centroids, candidates):
    row_count = lax.axis_size("row")
    ctr_count = lax.axis_size("ctr")
    ctr_place = lax.axis_index("ctr")
    blocks_held = centroids.shape[0]
    features = embeddings.shape[1]
    row_block = embeddings.shape[0]
    values = embeddings.astype(jnp.float32)
    normed = (
        values * lax.rsqrt(jnp.mean(values * values, axis=-1, keepdims=True) + epsilon)
    ).astype(jnp.bfloat16)
    owner_range = jnp.arange(row_count)
    group_lists = lax.all_gather(candidates, "ctr", axis=0, tiled=True)
    owners_here = group_lists // blocks_held
    matches = owners_here[:, :, None] == owner_range
    request = jnp.max(jnp.where(matches, (group_lists % blocks_held)[:, :, None], -1), axis=(0, 1))
    wanted = lax.all_to_all(request[:, None], "row", split_axis=0, concat_axis=0, tiled=True)[:, 0]
    owner_of = group_lists // blocks_held
    slot_map = (owner_of[:, :, None] == owner_range).astype(jnp.float32)
    ownership_map = (wanted[:, None] == jnp.arange(blocks_held)).astype(jnp.bfloat16)
    outgoing = jnp.take(centroids, jnp.maximum(wanted, 0), axis=0)
    fetched = lax.all_to_all(outgoing, "row", split_axis=0, concat_axis=0, tiled=True)
    picked = jnp.take(fetched, owner_of, axis=0)
    every_row = lax.all_gather(normed, "ctr", axis=0, tiled=True).reshape(
        ctr_count, row_block, features
    )
    scores = score_scale * jnp.einsum(
        "qrd,qjkd->qjkr", every_row, picked, preferred_element_type=jnp.float32
    )
    local_max = jnp.max(scores, axis=(1, 2))
    local_sum = jnp.sum(jnp.exp(scores - local_max[:, None, None, :]), axis=(1, 2))
    highest = lax.pmax(local_max, "ctr")
    soft_total = lax.psum(local_sum * jnp.exp(local_max - highest), "ctr")
    weights = (jnp.exp(scores - highest[:, None, None, :]) / soft_total[:, None, None, :]).astype(
        jnp.bfloat16
    )
    contribution = jnp.einsum(
        "qjkr,qrd->qjkd", weights, every_row, preferred_element_type=jnp.float32
    )
    partial_value = jnp.einsum(
        "qjo,qjkd->okd", slot_map, contribution, precision=lax.Precision.HIGHEST
    ).astype(jnp.bfloat16)
    returned_value = lax.all_to_all(partial_value, "row", split_axis=0, concat_axis=0, tiled=True)
    running_totals = jnp.einsum(
        "en,erv->nrv", ownership_map, returned_value, preferred_element_type=jnp.float32
    )
    renewed = (
        running_totals
        * lax.rsqrt(jnp.mean(running_totals * running_totals, axis=-1, keepdims=True) + epsilon)
        / math.sqrt(features)
    ).astype(jnp.bfloat16)
    refreshed = lax.all_to_all(
        jnp.take(renewed, jnp.maximum(wanted, 0), axis=0),
        "row",
        split_axis=0,
        concat_axis=0,
        tiled=True,
    )
    picked_new = jnp.take(refreshed, owner_of, axis=0)
    similar = jnp.einsum(
        "qrd,qjkd->qjkr", every_row, picked_new, preferred_element_type=jnp.float32
    )
    local_best = jnp.max(similar, axis=(1, 2))
    nearest = lax.pmax(local_best, "ctr")
    own_best = lax.dynamic_index_in_dim(nearest, ctr_place, 0, keepdims=False)
    return (renewed, own_best)


def solution(mesh):
    in_specs = (P(("row", "ctr"), None), P("row", "ctr", None), P(("row", "ctr"), None))
    out_specs = (P("row", "ctr", None), P(("row", "ctr")))
    return jax.shard_map(
        on_device, mesh=mesh, in_specs=in_specs, out_specs=out_specs, check_vma=False
    )
```

profile of v0, /device:TPU:0, one launch (start us, length us, event | category | flops | bytes accessed | tf_op | source)
XLA Modules:
  0.0 424.6 jit_solution(9521221970004577060)
XLA Ops:
  7.2 0.0 copy-start
  7.2 0.0 copy-start.3
  7.2 0.0 all-gather.3.cloned.1.call-start
  7.2 2.3 fusion.6
  9.6 3.5 fusion.7
  13.1 0.0 all-gather.3.cloned.1.call-update
  13.1 0.0 copy-done.3
  13.2 9.8 %all-gather = s32[4,1,6]{2,1,0:T(1,128)S(1)} all-gather(s32[1,1,6]{2,1,0:T(1,128)S(1)} %bitcast.29), channel_id=1, replica_groups=mesh['row'=32,'ctr'=4] {'ctr'}, dimensions={0}, use_global_device_ids=true | all-gather | bytes 120 | tf_op jit(solution)/shard_map/all_gather | solution.py:24
  22.9 0.1 select_reduce_fusion
  23.0 0.1 copy.15
  23.1 15.5 %all_to_all.24 = s32[32,1,1]{2,1,0:T(1,128)S(1)} all-to-all(s32[32,1,1]{2,1,0:T(1,128)S(1)} %copy.15), channel_id=1, replica_groups=mesh['row'=32,'ctr'=4] {'row'}, dimensions={0} | all-to-all | bytes 256 | tf_op jit(solution)/shard_map/all_to_all | solution.py:28
  38.6 0.7 reduce
  39.3 0.0 copy-done
  39.3 3.6 gather_fusion
  42.9 6.1 %broadcast_select_fusion.1 = bf16[32,64,1536]{2,1,0:T(8,128)(2,1)} fusion(bf16[32,64,1536]{2,1,0:T(8,128)(2,1)} %gather_fusion, pred[32]{0:T(512)(128)(4,1)S(1)} %broadcast_compare_fusion.1), kind=kLoop, calls=%fused_computation.12 | loop fusion | flops 3145728 | bytes 12582944 | tf_op jit(solution)/shard_map/jit(_take)/select_n | solution.py:32
  48.9 4.9 %all-to-all-start.1 = ((bf16[32,64,1536]{2,1,0:T(8,128)(2,1)}), bf16[32,64,1536]{2,1,0:T(8,128)(2,1)}, u32[]{:S(2)}, u32[]{:S(2)}) async-start(bf16[32,64,1536]{2,1,0:T(8,128)(2,1)} %broadcast_select_fusion.1), calls=%async_computation.1 | async-start | bytes 12582912 | tf_op jit(solution)/shard_map/all_to_all | solution.py:33
  53.9 0.1 reshape.86
  54.0 77.8 %all-to-all-done.1 = bf16[32,64,1536]{2,1,0:T(8,128)(2,1)} async-done(((bf16[32,64,1536]{2,1,0:T(8,128)(2,1)}), bf16[32,64,1536]{2,1,0:T(8,128)(2,1)}, u32[]{:S(2)}, u32[]{:S(2)}) %all-to-all-start.1) | async-done | bytes 6291488 | tf_op jit(solution)/shard_map/all_to_all | solution.py:33
  131.8 5.9 %gather_fusion.1 = bf16[24,64,1536]{2,1,0:T(8,128)(2,1)} fusion(bf16[32,64,1536]{2,1,0:T(8,128)(2,1)} %all-to-all-done.1, s32[1024]{0:T(1024)S(1)} %pad_clamp_fusion), kind=kCustom, calls=%fused_computation.1.clone | custom fusion | bytes 9437280 | tf_op jit(solution)/shard_map/jit(_take)/gather | solution.py:34
  137.7 0.0 all-gather.3.cloned.1.call-done
  137.7 11.2 %multiply_reduce_fusion.1 = (f32[4,768]{1,0:T(4,128)S(1)}, f32[4,6,64,768]{3,2,1,0:T(8,128)}) fusion(bf16[4,768,1536,1]{2,1,3,0:T(8,128)(2,1)} %bitcast.30, bf16[4,6,64,1536]{3,2,1,0:T(8,128)(2,1)} %bitcast.24, pred[4,6]{1,0:T(4,128)(4,1)S(1)} %get-tuple-element.12), kind=kOutput, calls=%fused_computation.25 | convolution fusion | flops 3628594176 | bytes 18886680 | tf_op jit(solution)/shard_map/qrd,qjkd->qjkr/dot_general | solution.py:38
  148.9 14.3 %pmax.14 = f32[4,768]{1,0:T(4,128)S(1)} all-reduce(f32[4,768]{1,0:T(4,128)S(1)} %get-tuple-element.14), channel_id=1, replica_groups=mesh['row'=32,'ctr'=4] {'ctr'}, use_global_device_ids=true, to_apply=%region_3.6 | all-reduce | flops 3072 | bytes 24576 | tf_op jit(solution)/shard_map/pmax | solution.py:43
  163.2 3.1 exponential_reduce_fusion
  166.3 15.3 %psum.7 = f32[4,768]{1,0:T(4,128)S(1)} all-reduce(f32[4,768]{1,0:T(4,128)S(1)} %exponential_multiply_fusion), channel_id=1, replica_groups=mesh['row'=32,'ctr'=4] {'ctr'}, use_global_device_ids=true, to_apply=%region_5.8 | all-reduce | flops 3072 | bytes 24576 | tf_op jit(solution)/shard_map/psum | solution.py:44
  181.6 7.8 %fusion.14 = f32[4,6,64,1536]{3,2,1,0:T(8,128)S(1)} fusion(bf16[4,768,1536,1]{2,1,3,0:T(8,128)(2,1)} %bitcast.31, f32[4,6,64,768]{3,2,1,0:T(8,128)} %get-tuple-element.15, f32[4,768]{1,0:T(4,128)S(1)} %psum.7, f32[4,768]{1,0:T(4,128)S(1)} %pmax.14), kind=kOutput, calls=%fused_computation.26 | convolution fusion | flops 3628597248 | bytes 23617536 | tf_op jit(solution)/shard_map/qjkr,qrd->qjkd/dot_general | solution.py:48
  189.5 16.4 %bitcast_convert_fusion = bf16[32,64,1536]{2,0,1:T(8,128)(2,1)S(1)} fusion(f32[4,6,64,1536]{3,2,1,0:T(8,128)S(1)} %fusion.14, s32[4,6]{1,0:T(4,128)S(1)} %get-tuple-element.13), kind=kOutput, calls=%fused_computation.4 | convolution fusion | flops 909116160 | bytes 15728736 | tf_op jit(solution)/shard_map/qjo,qjkd->okd/dot_general | solution.py:51
  205.8 3.5 copy.17
  209.3 76.6 %all_to_all.25 = bf16[32,64,1536]{2,1,0:T(8,128)(2,1)S(1)} all-to-all(bf16[32,64,1536]{2,1,0:T(8,128)(2,1)S(1)} %copy.17), channel_id=1, replica_groups=mesh['row'=32,'ctr'=4] {'row'}, dimensions={0} | all-to-all | bytes 12582912 | tf_op jit(solution)/shard_map/all_to_all | solution.py:54
  285.9 6.9 %multiply_reduce_fusion = (f32[16,64]{0,1:T(8,128)S(1)}, f32[16,64,1536]{2,0,1:T(8,128)S(1)}) fusion(bf16[32,64,1536]{2,1,0:T(8,128)(2,1)S(1)} %all_to_all.25, s32[32]{0:T(128)S(1)} %reduce), kind=kOutput, calls=%fused_computation.10 | convolution fusion | flops 103808512 | bytes 12587136 | tf_op jit(solution)/shard_map/en,erv->nrv/dot_general | solution.py:55
  292.8 0.6 multiply_convert_fusion
  293.4 1.7 copy.20
  295.2 0.0 copy-start.2
  295.2 3.7 gather_fusion.2
  298.8 0.0 copy-done.2
  298.8 6.1 %broadcast_select_fusion = bf16[32,64,1536]{2,1,0:T(8,128)(2,1)} fusion(bf16[32,64,1536]{2,1,0:T(8,128)(2,1)} %gather_fusion.2, pred[32]{0:T(512)(128)(4,1)S(1)} %broadcast_compare_fusion.1), kind=kLoop, calls=%fused_computation.11 | loop fusion | flops 3145728 | bytes 12582944 | tf_op jit(solution)/shard_map/jit(_take)/select_n | solution.py:64
  304.9 5.3 %all-to-all-start.3 = ((bf16[32,64,1536]{2,1,0:T(8,128)(2,1)}), bf16[32,64,1536]{2,1,0:T(8,128)(2,1)}, u32[]{:S(2)}, u32[]{:S(2)}) async-start(bf16[32,64,1536]{2,1,0:T(8,128)(2,1)} %broadcast_select_fusion), calls=%async_computation.3 | async-start | bytes 12582912 | tf_op jit(solution)/shard_map/all_to_all | solution.py:63
  310.2 77.6 %all-to-all-done.3 = bf16[32,64,1536]{2,1,0:T(8,128)(2,1)} async-done(((bf16[32,64,1536]{2,1,0:T(8,128)(2,1)}), bf16[32,64,1536]{2,1,0:T(8,128)(2,1)}, u32[]{:S(2)}, u32[]{:S(2)}) %all-to-all-start.3) | async-done | bytes 6291488 | tf_op jit(solution)/shard_map/all_to_all | solution.py:63
  387.8 5.9 %gather_fusion.3 = bf16[24,64,1536]{2,1,0:T(8,128)(2,1)} fusion(bf16[32,64,1536]{2,1,0:T(8,128)(2,1)} %all-to-all-done.3, s32[1024]{0:T(1024)S(1)} %pad_clamp_fusion), kind=kCustom, calls=%fused_computation.3.clone | custom fusion | bytes 9437280 | tf_op jit(solution)/shard_map/jit(_take)/gather | solution.py:70
  393.7 0.0 copy-start.1
  393.7 9.1 %fusion.20 = f32[4,768]{1,0:T(4,128)S(1)} fusion(bf16[4,768,1536,1]{2,1,3,0:T(8,128)(2,1)} %bitcast.32, bf16[4,6,64,1536]{3,2,1,0:T(8,128)(2,1)} %bitcast.25, pred[4,6]{1,0:T(4,128)(4,1)S(1)} %get-tuple-element.12), kind=kOutput, calls=%fused_computation.32 | convolution fusion | flops 3627414528 | bytes 14168088 | tf_op jit(solution)/shard_map/qrd,qjkd->qjkr/dot_general | solution.py:71
  402.9 14.3 %pmax.15 = f32[4,768]{1,0:T(4,128)S(1)} all-reduce(f32[4,768]{1,0:T(4,128)S(1)} %fusion.20), channel_id=1, replica_groups=mesh['row'=32,'ctr'=4] {'ctr'}, use_global_device_ids=true, to_apply=%region_8.11 | all-reduce | flops 3072 | bytes 24576 | tf_op jit(solution)/shard_map/pmax | solution.py:75
  417.2 0.6 dynamic-slice_reduce_fusion
  417.8 0.0 copy-done.1
  (10 shorter events, 0.1 us)
Async XLA Ops:
  7.2 32.1 %copy-start = (bf16[16,64,1536]{2,1,0:T(8,128)(2,1)S(1)}, bf16[16,64,1536]{2,1,0:T(8,128)(2,1)}, u32[]{:S(2)}) copy-start(bf16[16,64,1536]{2,1,0:T(8,128)(2,1)} %param.8) | copy-start | bytes 9437188
  7.2 6.0 %copy-start.3 = (s32[1,6]{1,0:T(1,128)S(1)}, s32[1,6]{1,0:T(1,128)}, u32[]{:S(2)}) copy-start(s32[1,6]{1,0:T(1,128)} %param.9) | copy-start | bytes 76
  7.2 130.5 %all-gather.3.cloned.1.call-start = ((), (), s32[]{:S(2)}) async-start(), calls=%async_computation.4 | async-start | bytes 11796480 | tf_op jit(solution)/shard_map/all_gather | solution.py:35
  48.9 82.8 %all-to-all-start.1 = ((bf16[32,64,1536]{2,1,0:T(8,128)(2,1)}), bf16[32,64,1536]{2,1,0:T(8,128)(2,1)}, u32[]{:S(2)}, u32[]{:S(2)}) async-start(bf16[32,64,1536]{2,1,0:T(8,128)(2,1)} %broadcast_select_fusion.1), calls=%async_computation.1 | async-start | bytes 12582912 | tf_op jit(solution)/shard_map/all_to_all | solution.py:33
  295.2 3.7 copy-start.2
  304.9 82.9 %all-to-all-start.3 = ((bf16[32,64,1536]{2,1,0:T(8,128)(2,1)}), bf16[32,64,1536]{2,1,0:T(8,128)(2,1)}, u32[]{:S(2)}, u32[]{:S(2)}) async-start(bf16[32,64,1536]{2,1,0:T(8,128)(2,1)} %broadcast_select_fusion), calls=%async_computation.3 | async-start | bytes 12582912 | tf_op jit(solution)/shard_map/all_to_all | solution.py:63
  393.7 24.0 %copy-start.1 = (bf16[16,64,1536]{2,1,0:T(8,128)(2,1)S(1)}, bf16[16,64,1536]{2,1,0:T(8,128)(2,1)}, u32[]{:S(2)}) copy-start(bf16[16,64,1536]{2,1,0:T(8,128)(2,1)} %param.8) | copy-start | bytes 9437188
Sparse Core Ops, SparseCore 0:
  13.3 94.4 all-gather.2
where the time goes:
time: 425 us
  waiting for transfers between devices  155 us (36%)
  blocking collectives  146 us (34%)
  matrix products  51.4 us (12%)
  local copies, waits for them, and re-layouts  25 us (6%)
  other arithmetic  22.6 us (5%)
  between operations  14.2 us (3%)
  starting transfers between devices  10.3 us (2%)
    all_to_all x1, waiting for transfers between devices, on_device(): lax.all_to_all(outgoing, 'row', split_axis=0, concat_axis=0, tiled=True)  77.8 us
    all_to_all x1, waiting for transfers between devices, on_device(): lax.all_to_all(jnp.take(renewed, jnp.maximum(wanted, 0), axis=0), 'row',...  77.6 us
    all_to_all x1, blocking collectives, on_device(): lax.all_to_all(partial_value, 'row', split_axis=0, concat_axis=0, tiled=T...  76.6 us
    dot_general x1, matrix products, on_device(): jnp.einsum('qjo,qjkd->okd', slot_map, contribution, precision=lax.Precisi...  16.4 us
    all_to_all x1, blocking collectives, on_device(): lax.all_to_all(request[:, None], 'row', split_axis=0, concat_axis=0, tile...  15.5 us
    psum x1, blocking collectives, on_device(): soft_total = lax.psum(local_sum * jnp.exp(local_max - highest), 'ctr')  15.3 us
    pmax x1, blocking collectives, on_device(): nearest = lax.pmax(local_best, 'ctr')  14.3 us
    pmax x1, blocking collectives, on_device(): highest = lax.pmax(local_max, 'ctr')  14.3 us
  transfers between devices with their start and end apart: 3, of which 2 were waited for; matrix products, arithmetic and copies ran while one was open for 4% of the time, Pallas kernels for 0%

commit v1 on v0

v1 whole, which is shorter than its diff:
```python
import functools
import math

import jax
import jax.numpy as jnp
from jax import lax
from jax.experimental import pallas as pl
from jax.experimental.pallas import tpu as pltpu
from jax.sharding import PartitionSpec as P

score_scale = 1.5
epsilon = 1e-06
MESH = pl.DeviceIdType.MESH

N_Z, N_Y, N_C = 4, 4, 2
N_ROW = N_Z * N_Y * N_C
N_CTR = 4
CANDS = 6
PIECES = 4


def shifted(row, k, sign):
    z, y, c = row // 8, (row // 2) % 4, row % 2
    dz, dy, dc = k // 8, (k // 2) % 4, k % 2
    return (
        lax.rem(z + sign * dz + 4, 4) * 8
        + lax.rem(y + sign * dy + 4, 4) * 2
        + lax.rem(c + sign * dc + 2, 2)
    )


def kernel(
    wanted, slot_of, j_of, sorted_k, same, last,
    emb_in, cent_in,
    new_out, near_out,
    rows, cent, stage, back, b0, b1, b2, b3, c0, c1, c2, c3,
    ex, wts, stat, wb, cum, f0, f1, f2, f3, st, bb, rb,
    loc_sem, xs, xr, s1, r1, s2, r2, s3, r3, ss, sr, ns, nr, out_sem,
):
    row, ctr = lax.axis_index("row"), lax.axis_index("ctr")
    fetched = (b0, b1, b2, b3)
    landed = (c0, c1, c2, c3)
    fresh = (f0, f1, f2, f3)
    RB = rows.shape[0] // N_CTR
    D = rows.shape[1]
    H = cent.shape[1] // PIECES
    CB = cent.shape[1]
    Q = RB // 4

    emb_copy = pltpu.make_async_copy(emb_in, rows.at[pl.ds(0, RB)], loc_sem.at[0])
    cent_copy = pltpu.make_async_copy(cent_in, cent, loc_sem.at[1])
    emb_copy.start()
    cent_copy.start()

    barrier = pltpu.get_barrier_semaphore()

    def greet(k, carry):
        pl.semaphore_signal(
            barrier, inc=1, device_id=(shifted(row, k, 1), ctr), device_id_type=MESH
        )
        return carry

    lax.fori_loop(1, N_ROW, greet, 0)
    for d in range(1, N_CTR):
        pl.semaphore_signal(
            barrier, inc=1, device_id=(row, lax.rem(ctr + d, N_CTR)), device_id_type=MESH
        )
    pl.semaphore_wait(barrier, N_ROW - 1 + N_CTR - 1)

    right = (row, lax.rem(ctr + 1, N_CTR))
    left = (row, lax.rem(ctr + 3, N_CTR))

    def row_copy(src, dst, part, device, sem):
        return pltpu.make_async_remote_copy(
            src_ref=rows.at[pl.ds(src * RB + part * Q, Q)],
            dst_ref=rows.at[pl.ds(dst * RB + part * Q, Q)],
            send_sem=xs.at[sem],
            recv_sem=xr.at[sem],
            device_id=device,
            device_id_type=MESH,
        )

    to_right = [row_copy(0, 1, part, right, part) for part in range(4)]
    to_left = [row_copy(0, 3, part, left, 4 + part) for part in range(4)]
    onward = [
        row_copy(1, 2, 0, right, 8),
        row_copy(1, 2, 1, right, 9),
        row_copy(3, 2, 2, left, 10),
        row_copy(3, 2, 3, left, 11),
    ]

    emb_copy.wait()
    for one, two in zip((0, 1, 2, 3), (2, 3, 0, 1)):
        if one < 2:
            for part in (one, two):

                def normalise(t, carry):
                    place = pl.ds(pl.multiple_of(part * Q + t * 64, 64), 64)
                    values = rows[place, :].astype(jnp.float32)
                    scale = lax.rsqrt(jnp.mean(values * values, axis=-1, keepdims=True) + epsilon)
                    rows[place, :] = (values * scale).astype(jnp.bfloat16)
                    return carry

                lax.fori_loop(0, Q // 64, normalise, 0)
        to_right[one].start()
        to_left[two].start()

    def slot_send(src, dst, k, sign, send, recv):
        return pltpu.make_async_remote_copy(
            src_ref=src,
            dst_ref=dst,
            send_sem=send,
            recv_sem=recv,
            device_id=(shifted(row, k, sign), ctr),
            device_id_type=MESH,
        )

    def all_slots(buf_send, buf_recv, send, recv):
        others = pl.ds(1, N_ROW - 1)
        return pltpu.make_async_remote_copy(
            src_ref=buf_send.at[others],
            dst_ref=buf_recv.at[others],
            send_sem=send,
            recv_sem=recv,
            device_id=(row, ctr),
            device_id_type=MESH,
        )

    cent_copy.wait()
    for i in range(PIECES):

        def fetch(t, carry):
            k = lax.rem(t * 5, N_ROW)
            block = jnp.maximum(wanted[k], 0)
            stage[i, k] = cent[block, i * H : (i + 1) * H, :]

            @pl.when(k != 0)
            def _():
                slot_send(stage.at[i, k], fetched[i].at[k], k, 1, s1.at[i], r1.at[i]).start()

            return carry

        lax.fori_loop(0, N_ROW, fetch, 0)
        fetched[i][0] = stage[i, 0]

    to_right[0].wait_recv()
    onward[0].start()
    to_left[2].wait_recv()
    onward[2].start()
    to_right[1].wait_recv()
    onward[1].start()
    to_left[3].wait_recv()
    onward[3].start()
    for i in range(PIECES):
        done = all_slots(stage.at[i], fetched[i], s1.at[i], r1.at[i])
        done.wait_send()
        done.wait_recv()

    def scores_of(s):
        def pick(j, carry):
            slot = slot_of[s * CANDS + j]
            for i in range(PIECES):
                stat[pl.ds(pl.multiple_of(j * CB + i * H, H), H), :] = fetched[i][slot]
            return carry

        lax.fori_loop(0, CANDS, pick, 0)

        def tile(n, carry):
            place = pl.ds(pl.multiple_of(n * 256, 256), 256)
            near = pl.ds(pl.multiple_of(s * RB + n * 256, 256), 256)
            score = score_scale * lax.dot_general(
                stat[...], rows[near, :], (((1,), (1,)), ((), ())),
                preferred_element_type=jnp.float32,
            )
            top = jnp.max(score, axis=0, keepdims=True)
            power = jnp.exp(score - top)
            ex[s, :, place] = power
            st[0, s : s + 1, place] = top
            st[0, N_CTR + s : N_CTR + s + 1, place] = jnp.sum(power, axis=0, keepdims=True)
            return carry

        lax.fori_loop(0, RB // 256, tile, 0)

    scores_of(0)
    to_right[2].wait_recv()
    to_right[3].wait_recv()
    scores_of(1)
    to_left[0].wait_recv()
    to_left[1].wait_recv()
    scores_of(3)
    for copy in onward:
        copy.wait_recv()
    scores_of(2)
    for copy in to_right + to_left + onward:
        copy.wait_send()

    stat_sends = [
        pltpu.make_async_remote_copy(
            src_ref=st.at[0],
            dst_ref=st.at[d],
            send_sem=ss.at[d],
            recv_sem=sr.at[d],
            device_id=(row, lax.rem(ctr + d, N_CTR)),
            device_id_type=MESH,
        )
        for d in range(1, N_CTR)
    ]
    for copy in stat_sends:
        copy.start()
    for s in range(N_CTR):
        wts[s, CANDS] = jnp.zeros(wts.shape[2:], wts.dtype)
    for copy in stat_sends:
        copy.wait()
    for s in range(N_CTR):
        tops = [st[d, (s - d) % N_CTR : (s - d) % N_CTR + 1, :] for d in range(N_CTR)]
        totals = [
            st[d, N_CTR + (s - d) % N_CTR : N_CTR + (s - d) % N_CTR + 1, :] for d in range(N_CTR)
        ]
        highest = functools.reduce(jnp.maximum, tops)
        total = functools.reduce(
            jnp.add, [total * jnp.exp(top - highest) for top, total in zip(tops, totals)]
        )
        factor = jnp.exp(tops[0] - highest) / total

        def weigh(j, carry):
            place = pl.ds(pl.multiple_of(j * CB, CB), CB)
            wts[s, j] = (ex[s, place, :] * factor).astype(jnp.bfloat16)
            return carry

        lax.fori_loop(0, CANDS, weigh, 0)

    half = N_ROW // 2
    for i in range(PIECES):
        for h in range(2):

            def lay(t, carry):
                for s in range(N_CTR):
                    j = j_of[(h * half + t) * N_CTR + s]
                    wb[pl.ds(pl.multiple_of(t * H, H), H), s * RB : (s + 1) * RB] = wts[
                        s, j, i * H : (i + 1) * H, :
                    ]
                return carry

            lax.fori_loop(0, half, lay, 0)

            def multiply(n, carry):
                place = pl.ds(pl.multiple_of(n * 256, 256), 256)
                total = jnp.dot(wb[...], rows[:, place], preferred_element_type=jnp.float32)
                stage[i, h * half : (h + 1) * half, :, place] = total.reshape(half, H, 256).astype(
                    jnp.bfloat16
                )
                return carry

            lax.fori_loop(0, D // 256, multiply, 0)

            def deliver(t, carry):
                k = h * half + lax.rem(t * 5, half)

                @pl.when(k != 0)
                def _():
                    slot_send(stage.at[i, k], landed[i].at[k], k, -1, s2.at[i], r2.at[i]).start()

                return carry

            lax.fori_loop(0, half, deliver, 0)
        landed[i][0] = stage[i, 0]

    out_copies = []
    for i in range(PIECES):
        all_slots(stage.at[i], landed[i], s2.at[i], r2.at[i]).wait_recv()

        def add(t, total):
            keep = same[t].astype(jnp.float32)
            total = landed[i][sorted_k[t]].astype(jnp.float32) + total * keep
            cum[t] = total
            return total

        lax.fori_loop(0, N_ROW, add, jnp.zeros((H, D), jnp.float32))

        def renew(b, carry):
            end = last[b]
            total = cum[jnp.maximum(end, 0)]
            total = jnp.where(end >= 0, total, jnp.zeros_like(total))
            scale = lax.rsqrt(jnp.mean(total * total, axis=-1, keepdims=True) + epsilon)
            fresh[i][b] = (total * scale * (1.0 / math.sqrt(D))).astype(jnp.bfloat16)
            return carry

        lax.fori_loop(0, cent.shape[0], renew, 0)

        def give(t, carry):
            k = lax.rem(t * 5, N_ROW)
            back[i, k] = fresh[i][jnp.maximum(wanted[k], 0)]

            @pl.when(k != 0)
            def _():
                slot_send(back.at[i, k], fetched[i].at[k], k, 1, s3.at[i], r3.at[i]).start()

            return carry

        lax.fori_loop(0, N_ROW, give, 0)
        fetched[i][0] = back[i, 0]
        out = pltpu.make_async_copy(
            fresh[i], new_out.at[:, pl.ds(i * H, H)], out_sem.at[i]
        )
        out.start()
        out_copies.append(out)

    for i in range(PIECES):
        all_slots(back.at[i], fetched[i], s3.at[i], r3.at[i]).wait_recv()
        for s in range(N_CTR):
            for j in range(CANDS):
                stat[j * H : (j + 1) * H, :] = fetched[i][slot_of[s * CANDS + j]]

            def tile(n, carry):
                place = pl.ds(pl.multiple_of(n * 256, 256), 256)
                near = pl.ds(pl.multiple_of(s * RB + n * 256, 256), 256)
                similar = lax.dot_general(
                    stat[0 : CANDS * H, :], rows[near, :], (((1,), (1,)), ((), ())),
                    preferred_element_type=jnp.float32,
                )
                best = jnp.max(similar, axis=0, keepdims=True)
                if i > 0:
                    best = jnp.maximum(best, bb[s, 0:1, place])
                bb[s, :, place] = jnp.broadcast_to(best, (8, 256))
                return carry

            lax.fori_loop(0, RB // 256, tile, 0)
    best_sends = [
        pltpu.make_async_remote_copy(
            src_ref=bb.at[d],
            dst_ref=rb.at[d],
            send_sem=ns.at[d],
            recv_sem=nr.at[d],
            device_id=(row, lax.rem(ctr - d + N_CTR, N_CTR)),
            device_id_type=MESH,
        )
        for d in range(1, N_CTR)
    ]
    for copy in best_sends:
        copy.start()
    for i in range(PIECES):
        all_slots(stage.at[i], landed[i], s2.at[i], r2.at[i]).wait_send()
        all_slots(back.at[i], fetched[i], s3.at[i], r3.at[i]).wait_send()
        out_copies[i].wait()
    for copy in best_sends:
        copy.wait()
    best = bb[0, 0:1, :]
    for d in range(1, N_CTR):
        best = jnp.maximum(best, rb[d, 0:1, :])
    near_out[...] = best


def tables(candidates, blocks_held):
    row, ctr = lax.axis_index("row"), lax.axis_index("ctr")
    lists = lax.all_gather(candidates, ("row", "ctr"), axis=0, tiled=True).reshape(
        N_ROW, N_CTR, CANDS
    )
    ks = jnp.arange(N_ROW, dtype=jnp.int32)
    ahead, behind = shifted(row, ks, 1), shifted(row, ks, -1)
    asking = jnp.where(lists // blocks_held == row, lists % blocks_held, -1).max(axis=(1, 2))
    wanted = jnp.sum(jnp.where(ahead[:, None] == ks, asking[None, :] + 1, 0), axis=1) - 1
    mine = lax.dynamic_index_in_dim(lists, row, 0, keepdims=False) // blocks_held
    turn = (ctr - jnp.arange(N_CTR)) % N_CTR
    mine = jnp.sum(jnp.where(turn[:, None, None] == jnp.arange(N_CTR)[:, None], mine[None], 0), axis=1)
    hit = mine[:, :, None] == behind
    slot_of = jnp.sum(jnp.where(hit, ks, 0), axis=2).reshape(-1)
    js = jnp.arange(CANDS, dtype=jnp.int32)[None, :, None]
    j_of = CANDS + jnp.sum(jnp.where(hit, js - CANDS, 0), axis=1).T.reshape(-1)
    key = jnp.where(wanted < 0, blocks_held, wanted) * N_ROW + ks
    rank = jnp.sum((key[None, :] < key[:, None]).astype(jnp.int32), axis=1)
    at = rank[None, :] == ks[:, None]
    sorted_k = jnp.sum(jnp.where(at, ks, 0), axis=1)
    sorted_w = jnp.sum(jnp.where(at, wanted, 0), axis=1)
    before = jnp.sum(jnp.where(rank[None, :] == ks[:, None] - 1, wanted, 0), axis=1)
    same = jnp.logical_and(sorted_w == before, ks > 0).astype(jnp.int32)
    blocks = jnp.arange(blocks_held, dtype=jnp.int32)
    named = wanted[None, :] == blocks[:, None]
    last = jnp.max(jnp.where(named, rank[None, :], -1), axis=1)
    return [t.astype(jnp.int32) for t in (wanted, slot_of, j_of, sorted_k, same, last)]


def on_device(embeddings, centroids, candidates):
    blocks, width, features = centroids.shape
    rb = embeddings.shape[0]
    held = width // PIECES
    info = tables(candidates, blocks)
    bf16, f32 = jnp.bfloat16, jnp.float32
    piece = pltpu.VMEM((N_ROW, held, features), bf16)
    dma = pltpu.SemaphoreType.DMA
    renewed, nearest = pl.pallas_call(
        kernel,
        out_shape=(
            jax.ShapeDtypeStruct(centroids.shape, bf16),
            jax.ShapeDtypeStruct((1, rb), f32),
        ),
        in_specs=[pl.BlockSpec(memory_space=pltpu.SMEM)] * 6
        + [pl.BlockSpec(memory_space=pl.ANY)] * 2,
        out_specs=(
            pl.BlockSpec(memory_space=pl.ANY),
            pl.BlockSpec(memory_space=pltpu.VMEM),
        ),
        scratch_shapes=[
            pltpu.VMEM((N_CTR * rb, features), bf16),
            pltpu.VMEM((blocks, width, features), bf16),
            pltpu.VMEM((PIECES, N_ROW, held, features), bf16),
            pltpu.VMEM((PIECES, N_ROW, held, features), bf16),
            *([piece] * 8),
            pltpu.VMEM((N_CTR, CANDS * width, rb), f32),
            pltpu.VMEM((N_CTR, CANDS + 1, width, rb), bf16),
            pltpu.VMEM((CANDS * width, features), bf16),
            pltpu.VMEM((N_ROW // 2 * held, N_CTR * rb), bf16),
            pltpu.VMEM((N_ROW, held, features), f32),
            *([pltpu.VMEM((blocks, held, features), bf16)] * 4),
            pltpu.VMEM((N_CTR, 2 * N_CTR, rb), f32),
            pltpu.VMEM((N_CTR, 8, rb), f32),
            pltpu.VMEM((N_CTR, 8, rb), f32),
            dma((2,)),
            dma((12,)),
            dma((12,)),
            *([dma((PIECES,))] * 6),
            *([dma((N_CTR,))] * 4),
            dma((PIECES,)),
        ],
        compiler_params=pltpu.CompilerParams(
            collective_id=0, has_side_effects=True, vmem_limit_bytes=60 * 2**20
        ),
    )(*info, embeddings, centroids)
    return renewed, nearest.reshape(rb)


def solution(mesh):
    in_specs = (P(("row", "ctr"), None), P("row", "ctr", None), P(("row", "ctr"), None))
    out_specs = (P("row", "ctr", None), P(("row", "ctr")))
    return jax.shard_map(
        on_device, mesh=mesh, in_specs=in_specs, out_specs=out_specs, check_vma=False
    )
```

time: 425 us -> 308 us (0.72)
  Pallas kernels: 0 us -> 247 us
  waiting for transfers between devices: 155 us -> 0 us
  blocking collectives: 146 us -> 47.2 us
  matrix products: 51.4 us -> 0 us
  local copies, waits for them, and re-layouts: 25 us -> 5.43 us
  other arithmetic: 22.6 us -> 4.21 us
  between operations: 14.2 us -> 0.75 us
  starting transfers between devices: 10.3 us -> 0 us
    pallas_call x0 -> x1, Pallas kernels: none -> 247 us  [on_device(): pl.pallas_call(kernel, out_shape=(jax.ShapeDtypeStruct(centroids.shape, b...]
    all_to_all x2 -> x0, waiting for transfers between devices: 155 us -> none  [the longest x1 77.8 us: on_device(): lax.all_to_all(outgoing, 'row', split_axis=0, concat_axis=0, tiled=True)]
    all_to_all x2 -> x0, blocking collectives: 92 us -> none  [the longest x1 76.6 us: on_device(): lax.all_to_all(partial_value, 'row', split_axis=0, concat_axis=0, tiled=T...]
    dot_general x5 -> x0, matrix products: 51.4 us -> none  [the longest x1 16.4 us: on_device(): jnp.einsum('qjo,qjkd->okd', slot_map, contribution, precision=lax.Precisi...]
    all_gather x1, blocking collectives: 9.75 us -> 47.2 us  [tables(): lax.all_gather(candidates, ('row', 'ctr'), axis=0, tiled=True)]
    pmax x2 -> x0, blocking collectives: 28.6 us -> none  [the longest x1 14.3 us: on_device(): nearest = lax.pmax(local_best, 'ctr')]
    gather x4 -> x0, local copies, waits for them, and re-layouts: 19 us -> none  [the longest x1 5.89 us: on_device(): picked = jnp.take(fetched, owner_of, axis=0)]
    psum x1 -> x0, blocking collectives: 15.3 us -> none  [on_device(): soft_total = lax.psum(local_sum * jnp.exp(local_max - highest), 'ctr')]
  transfers between devices with their start and end apart: 3 -> 0, of which waited for: 2 -> 0; matrix products, arithmetic and copies ran while one was open for 4% -> 0% of each run, Pallas kernels for 0% -> 0%
where the time goes in v1:
time: 308 us; the launch traced here: 305 us
  Pallas kernels  247 us (80%)
  blocking collectives  47.2 us (15%)
  local copies, waits for them, and re-layouts  5.43 us (2%)
  other arithmetic  4.21 us (1%)
    pallas_call x1, Pallas kernels, on_device(): pl.pallas_call(kernel, out_shape=(jax.ShapeDtypeStruct(centroids.shape, b...  247 us
    all_gather x1, blocking collectives, tables(): lax.all_gather(candidates, ('row', 'ctr'), axis=0, tiled=True)  47.2 us

profile of v1, /device:TPU:0, one launch (start us, length us, event | category | flops | bytes accessed | tf_op | source)
XLA Modules:
  0.0 305.0 jit_solution(7607998791944854193)
XLA Ops:
  0.7 0.1 iota_compare_fusion.3
  0.8 47.2 %all-gather = s32[128,1,6]{2,1,0:T(1,128)S(1)} all-gather(s32[1,1,6]{2,1,0:T(1,128)} %bitcast.9), channel_id=1, replica_groups=mesh['row'=32,'ctr'=4] {'row','ctr'}, dimensions={0}, use_global_device_ids=true | all-gather | bytes 3096 | tf_op jit(solution)/shard_map/all_gather | solution.py:355
  47.9 0.1 fusion.2
  48.1 0.1 select_reduce_fusion.5
  48.2 0.1 copy.5
  48.3 0.2 fusion.6
  48.6 0.1 copy.6
  48.7 0.6 reshape.232.slot_of
  49.2 0.1 copy.7
  49.3 0.6 add.296.j_of
  50.0 0.1 reduce_max.26
  50.1 0.1 reduce_max.27
  50.2 0.2 select_reduce_fusion.3
  50.4 0.0 copy-start
  50.4 0.2 convert_reduce_fusion
  50.6 0.6 select_reduce_fusion.4.last
  51.2 0.7 select_reduce_fusion
  51.9 0.5 and_convert_fusion.same
  52.4 0.0 copy-done
  52.4 247.5 %shard_map.50 = (bf16[16,64,1536]{2,1,0:T(8,128)(2,1)}, f32[1,768]{1,0:T(1,128)}) custom-call(s32[32]{0:T(128)} %copy-done, s32[24]{0:T(128)} %reshape.232.slot_of, s32[128]{0:T(128)} %add.296.j_of, s32[32]{0:T(128)} %get-tuple-element.10.sorted_k, s32[32]{0:T(128)} %and_convert_fusion.same, s32[16]{0:T(128)} %select_reduce_fusion.4.last, ...), custom_call_target="tpu_custom_call" | custom-call | tf_op jit(solution)/shard_map/pallas_call | solution.py:390
  299.9 1.3 reduce.2
  301.2 3.8 %copy.9 = bf16[16,64,1536]{2,1,0:T(8,128)(2,1)} copy(bf16[16,64,1536]{2,1,0:T(8,128)(2,1)} %get-tuple-element.17) | data formatting | bytes 6291456
  (8 shorter events, 0.1 us)
Async XLA Ops:
  50.4 2.0 copy-start

commit v2 on v1

--- a/solution.py
+++ b/solution.py
@@ -29,13 +29,19 @@
     )
 
 
+def steps_from(owner, row):
+    dz = (row // 8 - owner // 8 + 4) % 4
+    dy = ((row // 2) % 4 - (owner // 2) % 4 + 4) % 4
+    dc = (row % 2 - owner % 2 + 2) % 2
+    return dz * 8 + dy * 2 + dc
+
+
 def kernel(
-    wanted, slot_of, j_of, sorted_k, same, last,
-    emb_in, cent_in,
+    lists, emb_in, cent_in,
     new_out, near_out,
     rows, cent, stage, back, b0, b1, b2, b3, c0, c1, c2, c3,
-    ex, wts, stat, wb, cum, f0, f1, f2, f3, st, bb, rb,
-    loc_sem, xs, xr, s1, r1, s2, r2, s3, r3, ss, sr, ns, nr, out_sem,
+    ex, wts, stat, wb, cum, f0, f1, f2, f3, st, bb, rb, mine, ours, asks, info, ours_at, info_at,
+    loc_sem, ms, mr, gs, gr, xs, xr, s1, r1, s2, r2, s3, r3, ss, sr, ns, nr, out_sem,
 ):
     row, ctr = lax.axis_index("row"), lax.axis_index("ctr")
     fetched = (b0, b1, b2, b3)
@@ -67,6 +73,30 @@
         )
     pl.semaphore_wait(barrier, N_ROW - 1 + N_CTR - 1)
 
+    lane = lax.broadcasted_iota(jnp.int32, (8, 128), 1)
+    line = lax.broadcasted_iota(jnp.int32, (8, 128), 0)
+    held = cent.shape[0]
+    tile = jnp.where(line == 1, CANDS, jnp.where(line == 0, -1, 0))
+    for j in range(CANDS):
+        owner, block = lists[0, j] // held, lists[0, j] % held
+        tile = jnp.where(jnp.logical_and(line == 0, lane == owner), block, tile)
+        tile = jnp.where(jnp.logical_and(line == 1, lane == owner), j, tile)
+        tile = jnp.where(jnp.logical_and(line == 2, lane == j), steps_from(owner, row), tile)
+    ours[0] = tile
+    list_sends = [
+        pltpu.make_async_remote_copy(
+            src_ref=ours.at[0],
+            dst_ref=ours.at[d],
+            send_sem=ms.at[d],
+            recv_sem=mr.at[d],
+            device_id=(row, lax.rem(ctr + d, N_CTR)),
+            device_id_type=MESH,
+        )
+        for d in range(1, N_CTR)
+    ]
+    for copy in list_sends:
+        copy.start()
+
     right = (row, lax.rem(ctr + 1, N_CTR))
     left = (row, lax.rem(ctr + 3, N_CTR))
 
@@ -89,21 +119,15 @@
         row_copy(3, 2, 3, left, 11),
     ]
 
-    emb_copy.wait()
-    for one, two in zip((0, 1, 2, 3), (2, 3, 0, 1)):
-        if one < 2:
-            for part in (one, two):
-
-                def normalise(t, carry):
-                    place = pl.ds(pl.multiple_of(part * Q + t * 64, 64), 64)
-                    values = rows[place, :].astype(jnp.float32)
-                    scale = lax.rsqrt(jnp.mean(values * values, axis=-1, keepdims=True) + epsilon)
-                    rows[place, :] = (values * scale).astype(jnp.bfloat16)
-                    return carry
-
-                lax.fori_loop(0, Q // 64, normalise, 0)
-        to_right[one].start()
-        to_left[two].start()
+    def normalise(part):
+        def some(t, carry):
+            place = pl.ds(pl.multiple_of(part * Q + t * 64, 64), 64)
+            values = rows[place, :].astype(jnp.float32)
+            scale = lax.rsqrt(jnp.mean(values * values, axis=-1, keepdims=True) + epsilon)
+            rows[place, :] = (values * scale).astype(jnp.bfloat16)
+            return carry
+
+        lax.fori_loop(0, Q // 64, some, 0)
 
     def slot_send(src, dst, k, sign, send, recv):
         return pltpu.make_async_remote_copy(
@@ -126,12 +150,73 @@
             device_id_type=MESH,
         )
 
+    emb_copy.wait()
+    normalise(0)
+    to_right[0].start()
+    normalise(2)
+    to_left[2].start()
+
+    for copy in list_sends:
+        copy.wait_recv()
+    mine[...] = functools.reduce(jnp.maximum, [ours[d] for d in range(N_CTR)])
+    asks[0] = mine[...]
+
+    def ask(t, carry):
+        k = t
+        slot_send(mine, asks.at[k], k, -1, gs.at[0], gr.at[0]).start()
+        return carry
+
+    lax.fori_loop(1, N_ROW, ask, 0)
+    ours_copy = pltpu.make_async_copy(ours, ours_at, loc_sem.at[2])
+    ours_copy.start()
+    normalise(1)
+    to_right[1].start()
+    normalise(3)
+    to_left[3].start()
+    for part in (2, 3):
+        to_right[part].start()
+        to_left[part - 2].start()
+
+    asked = pltpu.make_async_remote_copy(
+        src_ref=asks.at[pl.ds(1, N_ROW - 1)],
+        dst_ref=asks.at[pl.ds(1, N_ROW - 1)],
+        send_sem=gs.at[0],
+        recv_sem=gr.at[0],
+        device_id=(row, ctr),
+        device_id_type=MESH,
+    )
+    asked.wait_recv()
+    shape = (N_ROW, 128)
+    slot = lax.broadcasted_iota(jnp.int32, shape, 0)
+    column = lax.broadcasted_iota(jnp.int32, shape, 1)
+    table = asks[:, 0, :]
+    want = jnp.max(jnp.where(column == row, table, -1), axis=1, keepdims=True)
+    want = jnp.broadcast_to(want, shape)
+    want_row = jnp.max(jnp.where(column == slot, want, -1), axis=0, keepdims=True)
+    key = jnp.where(want < 0, held, want) * N_ROW + slot
+    key_row = jnp.max(jnp.where(column == slot, key, -1), axis=0, keepdims=True)
+    less = jnp.logical_and(key_row < key, column < N_ROW)
+    rank = jnp.sum(jnp.where(less, 1, 0), axis=1, keepdims=True)
+    at = rank == column
+    info[0:1, :] = want_row
+    info[1:2, :] = jnp.sum(jnp.where(at, slot, 0), axis=0, keepdims=True)
+    this = jnp.sum(jnp.where(at, want, 0), axis=0, keepdims=True)
+    before = jnp.sum(jnp.where(rank + 1 == column, want, 0), axis=0, keepdims=True)
+    after_first = lax.broadcasted_iota(jnp.int32, (1, 128), 1) > 0
+    info[2:3, :] = jnp.where(jnp.logical_and(this == before, after_first), 1, 0)
+    info[3:4, :] = jnp.max(jnp.where(want == column, rank, -1), axis=0, keepdims=True)
+    info[4:8, :] = jnp.zeros((4, 128), jnp.int32)
+    info_copy = pltpu.make_async_copy(info, info_at, loc_sem.at[3])
+    info_copy.start()
+    info_copy.wait()
+    ours_copy.wait()
+
     cent_copy.wait()
     for i in range(PIECES):
 
         def fetch(t, carry):
             k = lax.rem(t * 5, N_ROW)
-            block = jnp.maximum(wanted[k], 0)
+            block = jnp.maximum(info_at[0, k], 0)
             stage[i, k] = cent[block, i * H : (i + 1) * H, :]
 
             @pl.when(k != 0)
@@ -158,7 +243,7 @@
 
     def scores_of(s):
         def pick(j, carry):
-            slot = slot_of[s * CANDS + j]
+            slot = ours_at[s, 2, j]
             for i in range(PIECES):
                 stat[pl.ds(pl.multiple_of(j * CB + i * H, H), H), :] = fetched[i][slot]
             return carry
@@ -191,8 +276,9 @@
     for copy in onward:
         copy.wait_recv()
     scores_of(2)
-    for copy in to_right + to_left + onward:
+    for copy in to_right + to_left + onward + list_sends:
         copy.wait_send()
+    asked.wait_send()
 
     stat_sends = [
         pltpu.make_async_remote_copy(
@@ -234,8 +320,9 @@
         for h in range(2):
 
             def lay(t, carry):
+                owner = shifted(row, h * half + t, -1)
                 for s in range(N_CTR):
-                    j = j_of[(h * half + t) * N_CTR + s]
+                    j = ours_at[s, 1, owner]
                     wb[pl.ds(pl.multiple_of(t * H, H), H), s * RB : (s + 1) * RB] = wts[
                         s, j, i * H : (i + 1) * H, :
                     ]
@@ -270,15 +357,15 @@
         all_slots(stage.at[i], landed[i], s2.at[i], r2.at[i]).wait_recv()
 
         def add(t, total):
-            keep = same[t].astype(jnp.float32)
-            total = landed[i][sorted_k[t]].astype(jnp.float32) + total * keep
+            keep = info_at[2, t].astype(jnp.float32)
+            total = landed[i][info_at[1, t]].astype(jnp.float32) + total * keep
             cum[t] = total
             return total
 
         lax.fori_loop(0, N_ROW, add, jnp.zeros((H, D), jnp.float32))
 
         def renew(b, carry):
-            end = last[b]
+            end = info_at[3, b]
             total = cum[jnp.maximum(end, 0)]
             total = jnp.where(end >= 0, total, jnp.zeros_like(total))
             scale = lax.rsqrt(jnp.mean(total * total, axis=-1, keepdims=True) + epsilon)
@@ -289,7 +376,7 @@
 
         def give(t, carry):
             k = lax.rem(t * 5, N_ROW)
-            back[i, k] = fresh[i][jnp.maximum(wanted[k], 0)]
+            back[i, k] = fresh[i][jnp.maximum(info_at[0, k], 0)]
 
             @pl.when(k != 0)
             def _():
@@ -309,7 +396,7 @@
         all_slots(back.at[i], fetched[i], s3.at[i], r3.at[i]).wait_recv()
         for s in range(N_CTR):
             for j in range(CANDS):
-                stat[j * H : (j + 1) * H, :] = fetched[i][slot_of[s * CANDS + j]]
+                stat[j * H : (j + 1) * H, :] = fetched[i][ours_at[s, 2, j]]
 
             def tile(n, carry):
                 place = pl.ds(pl.multiple_of(n * 256, 256), 256)
@@ -347,43 +434,13 @@
     best = bb[0, 0:1, :]
     for d in range(1, N_CTR):
         best = jnp.maximum(best, rb[d, 0:1, :])
-    near_out[...] = best
-
-
-def tables(candidates, blocks_held):
-    row, ctr = lax.axis_index("row"), lax.axis_index("ctr")
-    lists = lax.all_gather(candidates, ("row", "ctr"), axis=0, tiled=True).reshape(
-        N_ROW, N_CTR, CANDS
-    )
-    ks = jnp.arange(N_ROW, dtype=jnp.int32)
-    ahead, behind = shifted(row, ks, 1), shifted(row, ks, -1)
-    asking = jnp.where(lists // blocks_held == row, lists % blocks_held, -1).max(axis=(1, 2))
-    wanted = jnp.sum(jnp.where(ahead[:, None] == ks, asking[None, :] + 1, 0), axis=1) - 1
-    mine = lax.dynamic_index_in_dim(lists, row, 0, keepdims=False) // blocks_held
-    turn = (ctr - jnp.arange(N_CTR)) % N_CTR
-    mine = jnp.sum(jnp.where(turn[:, None, None] == jnp.arange(N_CTR)[:, None], mine[None], 0), axis=1)
-    hit = mine[:, :, None] == behind
-    slot_of = jnp.sum(jnp.where(hit, ks, 0), axis=2).reshape(-1)
-    js = jnp.arange(CANDS, dtype=jnp.int32)[None, :, None]
-    j_of = CANDS + jnp.sum(jnp.where(hit, js - CANDS, 0), axis=1).T.reshape(-1)
-    key = jnp.where(wanted < 0, blocks_held, wanted) * N_ROW + ks
-    rank = jnp.sum((key[None, :] < key[:, None]).astype(jnp.int32), axis=1)
-    at = rank[None, :] == ks[:, None]
-    sorted_k = jnp.sum(jnp.where(at, ks, 0), axis=1)
-    sorted_w = jnp.sum(jnp.where(at, wanted, 0), axis=1)
-    before = jnp.sum(jnp.where(rank[None, :] == ks[:, None] - 1, wanted, 0), axis=1)
-    same = jnp.logical_and(sorted_w == before, ks > 0).astype(jnp.int32)
-    blocks = jnp.arange(blocks_held, dtype=jnp.int32)
-    named = wanted[None, :] == blocks[:, None]
-    last = jnp.max(jnp.where(named, rank[None, :], -1), axis=1)
-    return [t.astype(jnp.int32) for t in (wanted, slot_of, j_of, sorted_k, same, last)]
+    near_out[...] = best.reshape(near_out.shape)
 
 
 def on_device(embeddings, centroids, candidates):
     blocks, width, features = centroids.shape
     rb = embeddings.shape[0]
     held = width // PIECES
-    info = tables(candidates, blocks)
     bf16, f32 = jnp.bfloat16, jnp.float32
     piece = pltpu.VMEM((N_ROW, held, features), bf16)
     dma = pltpu.SemaphoreType.DMA
@@ -391,9 +448,9 @@
         kernel,
         out_shape=(
             jax.ShapeDtypeStruct(centroids.shape, bf16),
-            jax.ShapeDtypeStruct((1, rb), f32),
+            jax.ShapeDtypeStruct((rb,), f32),
         ),
-        in_specs=[pl.BlockSpec(memory_space=pltpu.SMEM)] * 6
+        in_specs=[pl.BlockSpec(memory_space=pltpu.SMEM)]
         + [pl.BlockSpec(memory_space=pl.ANY)] * 2,
         out_specs=(
             pl.BlockSpec(memory_space=pl.ANY),
@@ -414,7 +471,17 @@
             pltpu.VMEM((N_CTR, 2 * N_CTR, rb), f32),
             pltpu.VMEM((N_CTR, 8, rb), f32),
             pltpu.VMEM((N_CTR, 8, rb), f32),
-            dma((2,)),
+            pltpu.VMEM((8, 128), jnp.int32),
+            pltpu.VMEM((N_CTR, 8, 128), jnp.int32),
+            pltpu.VMEM((N_ROW, 8, 128), jnp.int32),
+            pltpu.VMEM((8, 128), jnp.int32),
+            pltpu.SMEM((N_CTR, 8, 128), jnp.int32),
+            pltpu.SMEM((8, 128), jnp.int32),
+            dma((4,)),
+            dma((N_CTR,)),
+            dma((N_CTR,)),
+            dma((1,)),
+            dma((1,)),
             dma((12,)),
             dma((12,)),
             *([dma((PIECES,))] * 6),
@@ -424,8 +491,8 @@
         compiler_params=pltpu.CompilerParams(
             collective_id=0, has_side_effects=True, vmem_limit_bytes=60 * 2**20
         ),
-    )(*info, embeddings, centroids)
-    return renewed, nearest.reshape(rb)
+    )(candidates, embeddings, centroids)
+    return renewed, nearest
 
 
 def solution(mesh):

time: 308 us -> 267 us (0.87)
  blocking collectives: 47.2 us -> 0 us
  Pallas kernels: 247 us -> 259 us
  other arithmetic: 4.21 us -> 0 us
    all_gather x1 -> x0, blocking collectives: 47.2 us -> none  [tables(): lax.all_gather(candidates, ('row', 'ctr'), axis=0, tiled=True)]
    pallas_call x1, Pallas kernels: 247 us -> 259 us  [on_device(): pl.pallas_call(kernel, out_shape=(jax.ShapeDtypeStruct(centroids.shape, b...]
where the time goes in v2:
time: 267 us; the launch traced here: 264 us
  Pallas kernels  259 us (97%)
  local copies, waits for them, and re-layouts  4.43 us (2%)
    pallas_call x1, Pallas kernels, on_device(): pl.pallas_call(kernel, out_shape=(jax.ShapeDtypeStruct(centroids.shape, b...  259 us

profile of v2, /device:TPU:0, one launch (start us, length us, event | category | flops | bytes accessed | tf_op | source)
XLA Modules:
  0.0 264.2 jit_solution(16890154918607531412)
XLA Ops:
  0.6 259.1 %shard_map.50 = (bf16[16,64,1536]{2,1,0:T(8,128)(2,1)}, f32[768]{0:T(1024)}) custom-call(s32[1,6]{1,0:T(1,128)} %lists.1, bf16[768,1536]{1,0:T(8,128)(2,1)} %emb_in.1, bf16[16,64,1536]{2,1,0:T(8,128)(2,1)} %cent_in.1), custom_call_target="tpu_custom_call" | custom-call | tf_op jit(solution)/shard_map/pallas_call | solution.py:447
  259.8 0.0 copy-start
  259.8 3.8 %copy.7 = bf16[16,64,1536]{2,1,0:T(8,128)(2,1)} copy(bf16[16,64,1536]{2,1,0:T(8,128)(2,1)} %get-tuple-element.4) | data formatting | bytes 6291456
  263.6 0.0 copy-done
  263.6 0.6 copy.8
Async XLA Ops:
  259.8 3.8 %copy-start = (f32[768]{0:T(1024)S(1)}, f32[768]{0:T(1024)}, u32[]{:S(2)}) copy-start(f32[768]{0:T(1024)} %get-tuple-element.5) | copy-start | bytes 9220

commit v3 on v2

--- a/solution.py
+++ b/solution.py
@@ -29,18 +29,22 @@
     )
 
 
-def steps_from(owner, row):
+def steps(t):
+    return lax.rem(t * 5, N_ROW)
+
+
+def slot_from(owner, row):
     dz = (row // 8 - owner // 8 + 4) % 4
     dy = ((row // 2) % 4 - (owner // 2) % 4 + 4) % 4
     dc = (row % 2 - owner % 2 + 2) % 2
-    return dz * 8 + dy * 2 + dc
+    return (dz * 8 + dy * 2 + dc) * 13 % N_ROW
 
 
 def kernel(
     lists, emb_in, cent_in,
     new_out, near_out,
     rows, cent, stage, back, b0, b1, b2, b3, c0, c1, c2, c3,
-    ex, wts, stat, wb, cum, f0, f1, f2, f3, st, bb, rb, mine, ours, asks, info, ours_at, info_at,
+    ex, part, wts, stat, wb, cum, f0, f1, f2, f3, st, bb, rb, mine, ours, asks, info, ours_at, info_at,
     loc_sem, ms, mr, gs, gr, xs, xr, s1, r1, s2, r2, s3, r3, ss, sr, ns, nr, out_sem,
 ):
     row, ctr = lax.axis_index("row"), lax.axis_index("ctr")
@@ -51,7 +55,8 @@
     D = rows.shape[1]
     H = cent.shape[1] // PIECES
     CB = cent.shape[1]
-    Q = RB // 4
+    PARTS = 6
+    Q = RB // PARTS
 
     emb_copy = pltpu.make_async_copy(emb_in, rows.at[pl.ds(0, RB)], loc_sem.at[0])
     cent_copy = pltpu.make_async_copy(cent_in, cent, loc_sem.at[1])
@@ -71,7 +76,6 @@
         pl.semaphore_signal(
             barrier, inc=1, device_id=(row, lax.rem(ctr + d, N_CTR)), device_id_type=MESH
         )
-    pl.semaphore_wait(barrier, N_ROW - 1 + N_CTR - 1)
 
     lane = lax.broadcasted_iota(jnp.int32, (8, 128), 1)
     line = lax.broadcasted_iota(jnp.int32, (8, 128), 0)
@@ -81,8 +85,19 @@
         owner, block = lists[0, j] // held, lists[0, j] % held
         tile = jnp.where(jnp.logical_and(line == 0, lane == owner), block, tile)
         tile = jnp.where(jnp.logical_and(line == 1, lane == owner), j, tile)
-        tile = jnp.where(jnp.logical_and(line == 2, lane == j), steps_from(owner, row), tile)
+        tile = jnp.where(jnp.logical_and(line == 2, lane == j), slot_from(owner, row), tile)
     ours[0] = tile
+    emb_copy.wait()
+
+    def normalise(t, carry):
+        place = pl.ds(pl.multiple_of(t * 64, 64), 64)
+        values = rows[place, :].astype(jnp.float32)
+        scale = lax.rsqrt(jnp.mean(values * values, axis=-1, keepdims=True) + epsilon)
+        rows[place, :] = (values * scale).astype(jnp.bfloat16)
+        return carry
+
+    lax.fori_loop(0, RB // 64, normalise, 0)
+    pl.semaphore_wait(barrier, N_ROW - 1 + N_CTR - 1)
     list_sends = [
         pltpu.make_async_remote_copy(
             src_ref=ours.at[0],
@@ -100,34 +115,20 @@
     right = (row, lax.rem(ctr + 1, N_CTR))
     left = (row, lax.rem(ctr + 3, N_CTR))
 
-    def row_copy(src, dst, part, device, sem):
+    def row_copy(src, dst, p, device, sem):
         return pltpu.make_async_remote_copy(
-            src_ref=rows.at[pl.ds(src * RB + part * Q, Q)],
-            dst_ref=rows.at[pl.ds(dst * RB + part * Q, Q)],
+            src_ref=rows.at[pl.ds(src * RB + p * Q, Q)],
+            dst_ref=rows.at[pl.ds(dst * RB + p * Q, Q)],
             send_sem=xs.at[sem],
             recv_sem=xr.at[sem],
             device_id=device,
             device_id_type=MESH,
         )
 
-    to_right = [row_copy(0, 1, part, right, part) for part in range(4)]
-    to_left = [row_copy(0, 3, part, left, 4 + part) for part in range(4)]
-    onward = [
-        row_copy(1, 2, 0, right, 8),
-        row_copy(1, 2, 1, right, 9),
-        row_copy(3, 2, 2, left, 10),
-        row_copy(3, 2, 3, left, 11),
-    ]
-
-    def normalise(part):
-        def some(t, carry):
-            place = pl.ds(pl.multiple_of(part * Q + t * 64, 64), 64)
-            values = rows[place, :].astype(jnp.float32)
-            scale = lax.rsqrt(jnp.mean(values * values, axis=-1, keepdims=True) + epsilon)
-            rows[place, :] = (values * scale).astype(jnp.bfloat16)
-            return carry
-
-        lax.fori_loop(0, Q // 64, some, 0)
+    to_right = [row_copy(0, 1, p, right, p) for p in range(PARTS)]
+    to_left = [row_copy(0, 3, p, left, PARTS + p) for p in range(PARTS)]
+    onward = [row_copy(1, 2, p, right, 2 * PARTS + p) for p in range(PARTS // 2)]
+    onward += [row_copy(3, 2, p, left, 2 * PARTS + p) for p in range(PARTS // 2, PARTS)]
 
     def slot_send(src, dst, k, sign, send, recv):
         return pltpu.make_async_remote_copy(
@@ -135,7 +136,7 @@
             dst_ref=dst,
             send_sem=send,
             recv_sem=recv,
-            device_id=(shifted(row, k, sign), ctr),
+            device_id=(shifted(row, steps(k), sign), ctr),
             device_id_type=MESH,
         )
 
@@ -150,11 +151,9 @@
             device_id_type=MESH,
         )
 
-    emb_copy.wait()
-    normalise(0)
-    to_right[0].start()
-    normalise(2)
-    to_left[2].start()
+    for p in range(2):
+        to_right[p].start()
+        to_left[PARTS - 1 - p].start()
 
     for copy in list_sends:
         copy.wait_recv()
@@ -169,13 +168,9 @@
     lax.fori_loop(1, N_ROW, ask, 0)
     ours_copy = pltpu.make_async_copy(ours, ours_at, loc_sem.at[2])
     ours_copy.start()
-    normalise(1)
-    to_right[1].start()
-    normalise(3)
-    to_left[3].start()
-    for part in (2, 3):
-        to_right[part].start()
-        to_left[part - 2].start()
+    for p in range(2, PARTS):
+        to_right[p].start()
+        to_left[PARTS - 1 - p].start()
 
     asked = pltpu.make_async_remote_copy(
         src_ref=asks.at[pl.ds(1, N_ROW - 1)],
@@ -215,7 +210,7 @@
     for i in range(PIECES):
 
         def fetch(t, carry):
-            k = lax.rem(t * 5, N_ROW)
+            k = t
             block = jnp.maximum(info_at[0, k], 0)
             stage[i, k] = cent[block, i * H : (i + 1) * H, :]
 
@@ -228,24 +223,26 @@
         lax.fori_loop(0, N_ROW, fetch, 0)
         fetched[i][0] = stage[i, 0]
 
-    to_right[0].wait_recv()
-    onward[0].start()
-    to_left[2].wait_recv()
-    onward[2].start()
-    to_right[1].wait_recv()
-    onward[1].start()
-    to_left[3].wait_recv()
-    onward[3].start()
-    for i in range(PIECES):
-        done = all_slots(stage.at[i], fetched[i], s1.at[i], r1.at[i])
-        done.wait_send()
-        done.wait_recv()
-
-    def scores_of(s):
+    for p in range(PARTS // 2):
+        to_right[p].wait_recv()
+        onward[p].start()
+        to_left[PARTS - 1 - p].wait_recv()
+        onward[PARTS - 1 - p].start()
+    for p in range(PARTS // 2):
+        to_right[PARTS // 2 + p].wait_recv()
+        to_left[p].wait_recv()
+
+    AHEAD = PIECES - 1
+    G = CANDS * H
+
+    def scores_of(s, first, tiles):
+        lo, hi = (0, AHEAD) if first else (AHEAD, PIECES)
+        line = 0 if first else 2 * N_CTR
+
         def pick(j, carry):
             slot = ours_at[s, 2, j]
-            for i in range(PIECES):
-                stat[pl.ds(pl.multiple_of(j * CB + i * H, H), H), :] = fetched[i][slot]
+            for i in range(lo, hi):
+                stat[pl.ds(pl.multiple_of(i * G + j * H, H), H), :] = fetched[i][slot]
             return carry
 
         lax.fori_loop(0, CANDS, pick, 0)
@@ -254,31 +251,55 @@
             place = pl.ds(pl.multiple_of(n * 256, 256), 256)
             near = pl.ds(pl.multiple_of(s * RB + n * 256, 256), 256)
             score = score_scale * lax.dot_general(
-                stat[...], rows[near, :], (((1,), (1,)), ((), ())),
+                stat[lo * G : hi * G, :], rows[near, :], (((1,), (1,)), ((), ())),
                 preferred_element_type=jnp.float32,
             )
             top = jnp.max(score, axis=0, keepdims=True)
             power = jnp.exp(score - top)
-            ex[s, :, place] = power
-            st[0, s : s + 1, place] = top
-            st[0, N_CTR + s : N_CTR + s + 1, place] = jnp.sum(power, axis=0, keepdims=True)
+            ex[s, lo:hi, :, place] = power.reshape(hi - lo, G, 256)
+            part[line + s : line + s + 1, place] = top
+            part[line + N_CTR + s : line + N_CTR + s + 1, place] = jnp.sum(
+                power, axis=0, keepdims=True
+            )
             return carry
 
-        lax.fori_loop(0, RB // 256, tile, 0)
-
-    scores_of(0)
-    to_right[2].wait_recv()
-    to_right[3].wait_recv()
-    scores_of(1)
-    to_left[0].wait_recv()
-    to_left[1].wait_recv()
-    scores_of(3)
-    for copy in onward:
-        copy.wait_recv()
-    scores_of(2)
+        if len(tiles) == 1:
+            tile(tiles[0], 0)
+        else:
+            step = tiles[1] - tiles[0]
+            lax.fori_loop(0, len(tiles), lambda t, c: tile(tiles[0] + t * step, c), 0)
+
+    def fetch_done(i):
+        done = all_slots(stage.at[i], fetched[i], s1.at[i], r1.at[i])
+        done.wait_send()
+        done.wait_recv()
+
+    whole = range(RB // 256)
+    for i in range(AHEAD):
+        fetch_done(i)
+    for s in (0, 1, 3):
+        scores_of(s, True, whole)
+    for p in (0, 1, 4, 5):
+        onward[p].wait_recv()
+    scores_of(2, True, (0, 2))
+    fetch_done(AHEAD)
+    for s in (0, 1, 3):
+        scores_of(s, False, whole)
+    scores_of(2, False, (0, 2))
+    for p in (2, 3):
+        onward[p].wait_recv()
+    scores_of(2, True, (1,))
+    scores_of(2, False, (1,))
     for copy in to_right + to_left + onward + list_sends:
         copy.wait_send()
     asked.wait_send()
+
+    top_a, top_b = part[0:N_CTR, :], part[2 * N_CTR : 3 * N_CTR, :]
+    top = jnp.maximum(top_a, top_b)
+    st[0, 0:N_CTR, :] = top
+    st[0, N_CTR : 2 * N_CTR, :] = part[N_CTR : 2 * N_CTR, :] * jnp.exp(top_a - top) + part[
+        3 * N_CTR : 4 * N_CTR, :
+    ] * jnp.exp(top_b - top)
 
     stat_sends = [
         pltpu.make_async_remote_copy(
@@ -306,42 +327,48 @@
         total = functools.reduce(
             jnp.add, [total * jnp.exp(top - highest) for top, total in zip(tops, totals)]
         )
-        factor = jnp.exp(tops[0] - highest) / total
-
-        def weigh(j, carry):
-            place = pl.ds(pl.multiple_of(j * CB, CB), CB)
-            wts[s, j] = (ex[s, place, :] * factor).astype(jnp.bfloat16)
-            return carry
-
-        lax.fori_loop(0, CANDS, weigh, 0)
-
-    half = N_ROW // 2
+        for line in (0, 2 * N_CTR):
+            part[line + N_CTR + s : line + N_CTR + s + 1, :] = (
+                jnp.exp(part[line + s : line + s + 1, :] - highest) / total
+            )
+
     for i in range(PIECES):
-        for h in range(2):
+        line = N_CTR if i < AHEAD else 3 * N_CTR
+        for s in range(N_CTR):
+            factor = part[line + s : line + s + 1, :]
+
+            def weigh(j, carry):
+                place = pl.ds(pl.multiple_of(j * H, H), H)
+                wts[s, j] = (ex[s, i, place, :] * factor).astype(jnp.bfloat16)
+                return carry
+
+            lax.fori_loop(0, CANDS, weigh, 0)
+        batch = N_ROW // 4 if i == 0 else N_ROW // 2
+        for h in range(N_ROW // batch):
 
             def lay(t, carry):
-                owner = shifted(row, h * half + t, -1)
+                owner = shifted(row, steps(h * batch + t), -1)
                 for s in range(N_CTR):
                     j = ours_at[s, 1, owner]
-                    wb[pl.ds(pl.multiple_of(t * H, H), H), s * RB : (s + 1) * RB] = wts[
-                        s, j, i * H : (i + 1) * H, :
-                    ]
+                    wb[pl.ds(pl.multiple_of(t * H, H), H), s * RB : (s + 1) * RB] = wts[s, j]
                 return carry
 
-            lax.fori_loop(0, half, lay, 0)
+            lax.fori_loop(0, batch, lay, 0)
 
             def multiply(n, carry):
                 place = pl.ds(pl.multiple_of(n * 256, 256), 256)
-                total = jnp.dot(wb[...], rows[:, place], preferred_element_type=jnp.float32)
-                stage[i, h * half : (h + 1) * half, :, place] = total.reshape(half, H, 256).astype(
-                    jnp.bfloat16
+                total = jnp.dot(
+                    wb[0 : batch * H, :], rows[:, place], preferred_element_type=jnp.float32
                 )
+                stage[i, h * batch : (h + 1) * batch, :, place] = total.reshape(
+                    batch, H, 256
+                ).astype(jnp.bfloat16)
                 return carry
 
             lax.fori_loop(0, D // 256, multiply, 0)
 
             def deliver(t, carry):
-                k = h * half + lax.rem(t * 5, half)
+                k = h * batch + t
 
                 @pl.when(k != 0)
                 def _():
@@ -349,7 +376,7 @@
 
                 return carry
 
-            lax.fori_loop(0, half, deliver, 0)
+            lax.fori_loop(0, batch, deliver, 0)
         landed[i][0] = stage[i, 0]
 
     out_copies = []
@@ -375,7 +402,7 @@
         lax.fori_loop(0, cent.shape[0], renew, 0)
 
         def give(t, carry):
-            k = lax.rem(t * 5, N_ROW)
+            k = t
             back[i, k] = fresh[i][jnp.maximum(info_at[0, k], 0)]
 
             @pl.when(k != 0)
@@ -462,8 +489,9 @@
             pltpu.VMEM((PIECES, N_ROW, held, features), bf16),
             pltpu.VMEM((PIECES, N_ROW, held, features), bf16),
             *([piece] * 8),
-            pltpu.VMEM((N_CTR, CANDS * width, rb), f32),
-            pltpu.VMEM((N_CTR, CANDS + 1, width, rb), bf16),
+            pltpu.VMEM((N_CTR, PIECES, CANDS * held, rb), f32),
+            pltpu.VMEM((4 * N_CTR, rb), f32),
+            pltpu.VMEM((N_CTR, CANDS + 1, held, rb), bf16),
             pltpu.VMEM((CANDS * width, features), bf16),
             pltpu.VMEM((N_ROW // 2 * held, N_CTR * rb), bf16),
             pltpu.VMEM((N_ROW, held, features), f32),
@@ -482,8 +510,8 @@
             dma((N_CTR,)),
             dma((1,)),
             dma((1,)),
-            dma((12,)),
-            dma((12,)),
+            dma((18,)),
+            dma((18,)),
             *([dma((PIECES,))] * 6),
             *([dma((N_CTR,))] * 4),
             dma((PIECES,)),

time: 267 us -> 256 us (0.959)
  Pallas kernels: 259 us -> 251 us
    pallas_call x1, Pallas kernels: 259 us -> 251 us  [on_device(): pl.pallas_call(kernel, out_shape=(jax.ShapeDtypeStruct(centroids.shape, b...]
where the time goes in v3:
time: 256 us
  Pallas kernels  251 us (98%)
  local copies, waits for them, and re-layouts  4.43 us (2%)
    pallas_call x1, Pallas kernels, on_device(): pl.pallas_call(kernel, out_shape=(jax.ShapeDtypeStruct(centroids.shape, b...  251 us

profile of v3, /device:TPU:0, one launch (start us, length us, event | category | flops | bytes accessed | tf_op | source)
XLA Modules:
  0.0 255.8 jit_solution(11004662357084115043)
XLA Ops:
  0.6 250.7 %shard_map.50 = (bf16[16,64,1536]{2,1,0:T(8,128)(2,1)}, f32[768]{0:T(1024)}) custom-call(s32[1,6]{1,0:T(1,128)} %lists.1, bf16[768,1536]{1,0:T(8,128)(2,1)} %emb_in.1, bf16[16,64,1536]{2,1,0:T(8,128)(2,1)} %cent_in.1), custom_call_target="tpu_custom_call" | custom-call | tf_op jit(solution)/shard_map/pallas_call | solution.py:474
  251.4 0.0 copy-start
  251.4 3.8 %copy.7 = bf16[16,64,1536]{2,1,0:T(8,128)(2,1)} copy(bf16[16,64,1536]{2,1,0:T(8,128)(2,1)} %get-tuple-element.4) | data formatting | bytes 6291456
  255.2 0.0 copy-done
  255.2 0.6 copy.8
Async XLA Ops:
  251.4 3.8 %copy-start = (f32[768]{0:T(1024)S(1)}, f32[768]{0:T(1024)}, u32[]{:S(2)}) copy-start(f32[768]{0:T(1024)} %get-tuple-element.5) | copy-start | bytes 9220

commit v4 on v3

--- a/solution.py
+++ b/solution.py
@@ -56,6 +56,7 @@
     H = cent.shape[1] // PIECES
     CB = cent.shape[1]
     PARTS = 6
+    WIDE = D // 2
     Q = RB // PARTS
 
     emb_copy = pltpu.make_async_copy(emb_in, rows.at[pl.ds(0, RB)], loc_sem.at[0])
@@ -65,13 +66,16 @@
 
     barrier = pltpu.get_barrier_semaphore()
 
-    def greet(k, carry):
-        pl.semaphore_signal(
-            barrier, inc=1, device_id=(shifted(row, k, 1), ctr), device_id_type=MESH
-        )
-        return carry
-
-    lax.fori_loop(1, N_ROW, greet, 0)
+    z, y, c = row // 8, (row // 2) % 4, row % 2
+    z_at = [lax.rem(z + d, 4) * 8 for d in range(4)]
+    y_at = [lax.rem(y + d, 4) * 2 for d in range(4)]
+    c_at = [lax.rem(c + d, 2) for d in range(2)]
+
+    def ahead(k):
+        return z_at[k // 8] + y_at[(k // 2) % 4] + c_at[k % 2]
+
+    for k in range(1, N_ROW):
+        pl.semaphore_signal(barrier, inc=1, device_id=(ahead(k), ctr), device_id_type=MESH)
     for d in range(1, N_CTR):
         pl.semaphore_signal(
             barrier, inc=1, device_id=(row, lax.rem(ctr + d, N_CTR)), device_id_type=MESH
@@ -160,12 +164,17 @@
     mine[...] = functools.reduce(jnp.maximum, [ours[d] for d in range(N_CTR)])
     asks[0] = mine[...]
 
-    def ask(t, carry):
-        k = t
-        slot_send(mine, asks.at[k], k, -1, gs.at[0], gr.at[0]).start()
-        return carry
-
-    lax.fori_loop(1, N_ROW, ask, 0)
+    for t in range(1, N_ROW):
+        k = t * 5 % N_ROW
+        back_k = (4 - k // 8) % 4 * 8 + (4 - (k // 2) % 4) % 4 * 2 + k % 2
+        pltpu.make_async_remote_copy(
+            src_ref=mine,
+            dst_ref=asks.at[t],
+            send_sem=gs.at[0],
+            recv_sem=gr.at[0],
+            device_id=(ahead(back_k), ctr),
+            device_id_type=MESH,
+        ).start()
     ours_copy = pltpu.make_async_copy(ours, ours_at, loc_sem.at[2])
     ours_copy.start()
     for p in range(2, PARTS):
@@ -235,7 +244,7 @@
     AHEAD = PIECES - 1
     G = CANDS * H
 
-    def scores_of(s, first, tiles):
+    def scores_of(s, first, spans):
         lo, hi = (0, AHEAD) if first else (AHEAD, PIECES)
         line = 0 if first else 2 * N_CTR
 
@@ -247,49 +256,43 @@
 
         lax.fori_loop(0, CANDS, pick, 0)
 
-        def tile(n, carry):
-            place = pl.ds(pl.multiple_of(n * 256, 256), 256)
-            near = pl.ds(pl.multiple_of(s * RB + n * 256, 256), 256)
+        for start, width in spans:
+            place = pl.ds(start, width)
             score = score_scale * lax.dot_general(
-                stat[lo * G : hi * G, :], rows[near, :], (((1,), (1,)), ((), ())),
-                preferred_element_type=jnp.float32,
+                stat[lo * G : hi * G, :], rows[pl.ds(s * RB + start, width), :],
+                (((1,), (1,)), ((), ())), preferred_element_type=jnp.float32,
             )
             top = jnp.max(score, axis=0, keepdims=True)
             power = jnp.exp(score - top)
-            ex[s, lo:hi, :, place] = power.reshape(hi - lo, G, 256)
+            ex[s, lo:hi, :, place] = power.reshape(hi - lo, G, width)
             part[line + s : line + s + 1, place] = top
             part[line + N_CTR + s : line + N_CTR + s + 1, place] = jnp.sum(
                 power, axis=0, keepdims=True
             )
-            return carry
-
-        if len(tiles) == 1:
-            tile(tiles[0], 0)
-        else:
-            step = tiles[1] - tiles[0]
-            lax.fori_loop(0, len(tiles), lambda t, c: tile(tiles[0] + t * step, c), 0)
 
     def fetch_done(i):
         done = all_slots(stage.at[i], fetched[i], s1.at[i], r1.at[i])
         done.wait_send()
         done.wait_recv()
 
-    whole = range(RB // 256)
+    third = RB // 3
+    whole = [(0, RB)]
+    outer, middle = [(0, third), (2 * third, third)], [(third, third)]
     for i in range(AHEAD):
         fetch_done(i)
     for s in (0, 1, 3):
         scores_of(s, True, whole)
     for p in (0, 1, 4, 5):
         onward[p].wait_recv()
-    scores_of(2, True, (0, 2))
+    scores_of(2, True, outer)
     fetch_done(AHEAD)
     for s in (0, 1, 3):
         scores_of(s, False, whole)
-    scores_of(2, False, (0, 2))
+    scores_of(2, False, outer)
     for p in (2, 3):
         onward[p].wait_recv()
-    scores_of(2, True, (1,))
-    scores_of(2, False, (1,))
+    scores_of(2, True, middle)
+    scores_of(2, False, middle)
     for copy in to_right + to_left + onward + list_sends:
         copy.wait_send()
     asked.wait_send()
@@ -356,16 +359,16 @@
             lax.fori_loop(0, batch, lay, 0)
 
             def multiply(n, carry):
-                place = pl.ds(pl.multiple_of(n * 256, 256), 256)
+                place = pl.ds(pl.multiple_of(n * WIDE, WIDE), WIDE)
                 total = jnp.dot(
                     wb[0 : batch * H, :], rows[:, place], preferred_element_type=jnp.float32
                 )
                 stage[i, h * batch : (h + 1) * batch, :, place] = total.reshape(
-                    batch, H, 256
+                    batch, H, WIDE
                 ).astype(jnp.bfloat16)
                 return carry
 
-            lax.fori_loop(0, D // 256, multiply, 0)
+            lax.fori_loop(0, D // WIDE, multiply, 0)
 
             def deliver(t, carry):
                 k = h * batch + t
@@ -425,20 +428,14 @@
             for j in range(CANDS):
                 stat[j * H : (j + 1) * H, :] = fetched[i][ours_at[s, 2, j]]
 
-            def tile(n, carry):
-                place = pl.ds(pl.multiple_of(n * 256, 256), 256)
-                near = pl.ds(pl.multiple_of(s * RB + n * 256, 256), 256)
-                similar = lax.dot_general(
-                    stat[0 : CANDS * H, :], rows[near, :], (((1,), (1,)), ((), ())),
-                    preferred_element_type=jnp.float32,
-                )
-                best = jnp.max(similar, axis=0, keepdims=True)
-                if i > 0:
-                    best = jnp.maximum(best, bb[s, 0:1, place])
-                bb[s, :, place] = jnp.broadcast_to(best, (8, 256))
-                return carry
-
-            lax.fori_loop(0, RB // 256, tile, 0)
+            similar = lax.dot_general(
+                stat[0 : CANDS * H, :], rows[s * RB : (s + 1) * RB, :], (((1,), (1,)), ((), ())),
+                preferred_element_type=jnp.float32,
+            )
+            best = jnp.max(similar, axis=0, keepdims=True)
+            if i > 0:
+                best = jnp.maximum(best, bb[s, 0:1, :])
+            bb[s] = jnp.broadcast_to(best, bb.shape[1:])
     best_sends = [
         pltpu.make_async_remote_copy(
             src_ref=bb.at[d],
@@ -462,6 +459,21 @@
     for d in range(1, N_CTR):
         best = jnp.maximum(best, rb[d, 0:1, :])
     near_out[...] = best.reshape(near_out.shape)
+
+
+def hand_over(renewed, nearest, new_out, near_out, hold, near_hold, sems, outs):
+    blocks = renewed.shape[0]
+    ins = [pltpu.make_async_copy(renewed.at[b], hold.at[b], sems.at[b]) for b in range(blocks)]
+    ins.append(pltpu.make_async_copy(nearest, near_hold, sems.at[blocks]))
+    away = [pltpu.make_async_copy(hold.at[b], new_out.at[b], outs.at[b]) for b in range(blocks)]
+    away.append(pltpu.make_async_copy(near_hold, near_out, outs.at[blocks]))
+    for copy in ins:
+        copy.start()
+    for one, two in zip(ins, away):
+        one.wait()
+        two.start()
+    for copy in away:
+        copy.wait()
 
 
 def on_device(embeddings, centroids, candidates):
@@ -520,7 +532,21 @@
             collective_id=0, has_side_effects=True, vmem_limit_bytes=60 * 2**20
         ),
     )(candidates, embeddings, centroids)
-    return renewed, nearest
+    return pl.pallas_call(
+        hand_over,
+        out_shape=(
+            jax.ShapeDtypeStruct(centroids.shape, bf16),
+            jax.ShapeDtypeStruct((rb,), f32),
+        ),
+        in_specs=[pl.BlockSpec(memory_space=pl.ANY)] * 2,
+        out_specs=(pl.BlockSpec(memory_space=pl.ANY),) * 2,
+        scratch_shapes=[
+            pltpu.VMEM(centroids.shape, bf16),
+            pltpu.VMEM((rb,), f32),
+            dma((blocks + 1,)),
+            dma((blocks + 1,)),
+        ],
+    )(renewed, nearest)
 
 
 def solution(mesh):

time: 256 us -> 252 us (0.984)
  local copies, waits for them, and re-layouts: 4.43 us -> 0 us
    unnamed x4 -> x0, local copies, waits for them, and re-layouts: 4.43 us -> none
    pallas_call x1, Pallas kernels: 251 us -> 247 us  [on_device(): pl.pallas_call(kernel, out_shape=(jax.ShapeDtypeStruct(centroids.shape, b...]
    pallas_call x0 -> x1, Pallas kernels: none -> 3.19 us  [on_device(): pl.pallas_call(hand_over, out_shape=(jax.ShapeDtypeStruct(centroids.shape...]
where the time goes in v4:
time: 252 us; the launch traced here: 251 us
  Pallas kernels  251 us (100%)
    pallas_call x1, Pallas kernels, on_device(): pl.pallas_call(kernel, out_shape=(jax.ShapeDtypeStruct(centroids.shape, b...  247 us

profile of v4, /device:TPU:0, one launch (start us, length us, event | category | flops | bytes accessed | tf_op | source)
XLA Modules:
  0.0 251.4 jit_solution(5528426875989776135)
XLA Ops:
  0.6 247.4 %shard_map.50 = (bf16[16,64,1536]{2,1,0:T(8,128)(2,1)}, f32[768]{0:T(1024)}) custom-call(s32[1,6]{1,0:T(1,128)} %lists.1, bf16[768,1536]{1,0:T(8,128)(2,1)} %emb_in.1, bf16[16,64,1536]{2,1,0:T(8,128)(2,1)} %cent_in.1), custom_call_target="tpu_custom_call" | custom-call | tf_op jit(solution)/shard_map/pallas_call | solution.py:486
  248.0 3.2 %shard_map.51 = (bf16[16,64,1536]{2,1,0:T(8,128)(2,1)}, f32[768]{0:T(1024)}) custom-call(bf16[16,64,1536]{2,1,0:T(8,128)(2,1)} %get-tuple-element.4.renewed, f32[768]{0:T(1024)} %get-tuple-element.5.nearest), custom_call_target="tpu_custom_call" | custom-call | tf_op jit(solution)/shard_map/pallas_call | solution.py:535

commit v5 on v4

--- a/solution.py
+++ b/solution.py
@@ -43,12 +43,12 @@
 def kernel(
     lists, emb_in, cent_in,
     new_out, near_out,
-    rows, cent, stage, back, b0, b1, b2, b3, c0, c1, c2, c3,
+    rows, cent, stage, back, b0, b1, b2, b3, b4, c0, c1, c2, c3,
     ex, part, wts, stat, wb, cum, f0, f1, f2, f3, st, bb, rb, mine, ours, asks, info, ours_at, info_at,
     loc_sem, ms, mr, gs, gr, xs, xr, s1, r1, s2, r2, s3, r3, ss, sr, ns, nr, out_sem,
 ):
     row, ctr = lax.axis_index("row"), lax.axis_index("ctr")
-    fetched = (b0, b1, b2, b3)
+    fetched = (b0, b1, b2, b3, b4)
     landed = (c0, c1, c2, c3)
     fresh = (f0, f1, f2, f3)
     RB = rows.shape[0] // N_CTR
@@ -57,6 +57,8 @@
     CB = cent.shape[1]
     PARTS = 6
     WIDE = D // 2
+    units = [(i, 0, D) for i in range(PIECES - 1)]
+    units += [(PIECES - 1, 0, WIDE), (PIECES - 1, WIDE, D)]
     Q = RB // PARTS
 
     emb_copy = pltpu.make_async_copy(emb_in, rows.at[pl.ds(0, RB)], loc_sem.at[0])
@@ -145,15 +147,42 @@
         )
 
     def all_slots(buf_send, buf_recv, send, recv):
-        others = pl.ds(1, N_ROW - 1)
         return pltpu.make_async_remote_copy(
-            src_ref=buf_send.at[others],
-            dst_ref=buf_recv.at[others],
+            src_ref=buf_send,
+            dst_ref=buf_recv,
             send_sem=send,
             recv_sem=recv,
             device_id=(row, ctr),
             device_id_type=MESH,
         )
+
+    others = pl.ds(1, N_ROW - 1)
+
+    def unit_done(u, source, send, recv):
+        i, lo, hi = units[u]
+        return all_slots(
+            source.at[i, others, :, lo:hi], fetched[u].at[others], send.at[u], recv.at[u]
+        )
+
+    def sums_done(i):
+        return all_slots(stage.at[i, others], landed[i].at[others], s2.at[i], r2.at[i])
+
+    def unit_out(u, source, pick, send, recv):
+        i, lo, hi = units[u]
+
+        def one(k, carry):
+            source[i, k, :, lo:hi] = pick(i, k, lo, hi)
+
+            @pl.when(k != 0)
+            def _():
+                slot_send(
+                    source.at[i, k, :, lo:hi], fetched[u].at[k], k, 1, send.at[u], recv.at[u]
+                ).start()
+
+            return carry
+
+        lax.fori_loop(0, N_ROW, one, 0)
+        fetched[u][0] = source[i, 0, :, lo:hi]
 
     for p in range(2):
         to_right[p].start()
@@ -216,21 +245,11 @@
     ours_copy.wait()
 
     cent_copy.wait()
-    for i in range(PIECES):
-
-        def fetch(t, carry):
-            k = t
-            block = jnp.maximum(info_at[0, k], 0)
-            stage[i, k] = cent[block, i * H : (i + 1) * H, :]
-
-            @pl.when(k != 0)
-            def _():
-                slot_send(stage.at[i, k], fetched[i].at[k], k, 1, s1.at[i], r1.at[i]).start()
-
-            return carry
-
-        lax.fori_loop(0, N_ROW, fetch, 0)
-        fetched[i][0] = stage[i, 0]
+    def asked_block(i, k, lo, hi):
+        return cent[jnp.maximum(info_at[0, k], 0), i * H : (i + 1) * H, lo:hi]
+
+    for u in range(len(units)):
+        unit_out(u, stage, asked_block, s1, r1)
 
     for p in range(PARTS // 2):
         to_right[p].wait_recv()
@@ -244,24 +263,33 @@
     AHEAD = PIECES - 1
     G = CANDS * H
 
-    def scores_of(s, first, spans):
-        lo, hi = (0, AHEAD) if first else (AHEAD, PIECES)
-        line = 0 if first else 2 * N_CTR
+    def scores_of(s, step, spans):
+        lo, hi = (0, AHEAD) if step == 0 else (AHEAD, PIECES)
+        line = 0 if step == 0 else 2 * N_CTR
+        used = range(AHEAD) if step == 0 else [AHEAD + step - 1]
+        cols = slice(*units[used[0]][1:])
 
         def pick(j, carry):
             slot = ours_at[s, 2, j]
-            for i in range(lo, hi):
-                stat[pl.ds(pl.multiple_of(i * G + j * H, H), H), :] = fetched[i][slot]
+            for u in used:
+                place = pl.ds(pl.multiple_of(units[u][0] * G + j * H, H), H)
+                stat[place, cols] = fetched[u][slot]
             return carry
 
         lax.fori_loop(0, CANDS, pick, 0)
 
         for start, width in spans:
             place = pl.ds(start, width)
-            score = score_scale * lax.dot_general(
-                stat[lo * G : hi * G, :], rows[pl.ds(s * RB + start, width), :],
+            score = lax.dot_general(
+                stat[lo * G : hi * G, cols], rows[pl.ds(s * RB + start, width), cols],
                 (((1,), (1,)), ((), ())), preferred_element_type=jnp.float32,
             )
+            if step == 1:
+                ex[s, AHEAD, :, place] = score
+                continue
+            if step == 2:
+                score = score + ex[s, AHEAD, :, place]
+            score = score_scale * score
             top = jnp.max(score, axis=0, keepdims=True)
             power = jnp.exp(score - top)
             ex[s, lo:hi, :, place] = power.reshape(hi - lo, G, width)
@@ -270,8 +298,8 @@
                 power, axis=0, keepdims=True
             )
 
-    def fetch_done(i):
-        done = all_slots(stage.at[i], fetched[i], s1.at[i], r1.at[i])
+    def fetch_done(u):
+        done = unit_done(u, stage, s1, r1)
         done.wait_send()
         done.wait_recv()
 
@@ -281,18 +309,21 @@
     for i in range(AHEAD):
         fetch_done(i)
     for s in (0, 1, 3):
-        scores_of(s, True, whole)
+        scores_of(s, 0, whole)
     for p in (0, 1, 4, 5):
         onward[p].wait_recv()
-    scores_of(2, True, outer)
+    scores_of(2, 0, outer)
     fetch_done(AHEAD)
     for s in (0, 1, 3):
-        scores_of(s, False, whole)
-    scores_of(2, False, outer)
+        scores_of(s, 1, whole)
+    scores_of(2, 1, outer)
     for p in (2, 3):
         onward[p].wait_recv()
-    scores_of(2, True, middle)
-    scores_of(2, False, middle)
+    scores_of(2, 0, middle)
+    scores_of(2, 1, middle)
+    fetch_done(AHEAD + 1)
+    for s in range(N_CTR):
+        scores_of(s, 2, whole)
     for copy in to_right + to_left + onward + list_sends:
         copy.wait_send()
     asked.wait_send()
@@ -346,7 +377,7 @@
                 return carry
 
             lax.fori_loop(0, CANDS, weigh, 0)
-        batch = N_ROW // 4 if i == 0 else N_ROW // 2
+        batch = N_ROW // 2
         for h in range(N_ROW // batch):
 
             def lay(t, carry):
@@ -359,7 +390,7 @@
             lax.fori_loop(0, batch, lay, 0)
 
             def multiply(n, carry):
-                place = pl.ds(pl.multiple_of(n * WIDE, WIDE), WIDE)
+                place = pl.ds(n * WIDE, WIDE) if i == 0 else pl.ds(pl.multiple_of(n * WIDE, WIDE), WIDE)
                 total = jnp.dot(
                     wb[0 : batch * H, :], rows[:, place], preferred_element_type=jnp.float32
                 )
@@ -368,23 +399,33 @@
                 ).astype(jnp.bfloat16)
                 return carry
 
-            lax.fori_loop(0, D // WIDE, multiply, 0)
-
-            def deliver(t, carry):
-                k = h * batch + t
-
-                @pl.when(k != 0)
-                def _():
-                    slot_send(stage.at[i, k], landed[i].at[k], k, -1, s2.at[i], r2.at[i]).start()
-
-                return carry
-
-            lax.fori_loop(0, batch, deliver, 0)
+            def deliver(lo, hi):
+                def one(t, carry):
+                    k = h * batch + t
+
+                    @pl.when(k != 0)
+                    def _():
+                        slot_send(
+                            stage.at[i, k, :, lo:hi], landed[i].at[k, :, lo:hi], k, -1,
+                            s2.at[i], r2.at[i],
+                        ).start()
+
+                    return carry
+
+                lax.fori_loop(0, batch, one, 0)
+
+            if i == 0:
+                for n in range(D // WIDE):
+                    multiply(n, 0)
+                    deliver(n * WIDE, (n + 1) * WIDE)
+            else:
+                lax.fori_loop(0, D // WIDE, multiply, 0)
+                deliver(0, D)
         landed[i][0] = stage[i, 0]
 
     out_copies = []
     for i in range(PIECES):
-        all_slots(stage.at[i], landed[i], s2.at[i], r2.at[i]).wait_recv()
+        sums_done(i).wait_recv()
 
         def add(t, total):
             keep = info_at[2, t].astype(jnp.float32)
@@ -404,34 +445,32 @@
 
         lax.fori_loop(0, cent.shape[0], renew, 0)
 
-        def give(t, carry):
-            k = t
-            back[i, k] = fresh[i][jnp.maximum(info_at[0, k], 0)]
-
-            @pl.when(k != 0)
-            def _():
-                slot_send(back.at[i, k], fetched[i].at[k], k, 1, s3.at[i], r3.at[i]).start()
-
-            return carry
-
-        lax.fori_loop(0, N_ROW, give, 0)
-        fetched[i][0] = back[i, 0]
+        def renewed_block(i, k, lo, hi):
+            return fresh[i][jnp.maximum(info_at[0, k], 0), :, lo:hi]
+
+        for u in range(len(units)):
+            if units[u][0] == i:
+                unit_out(u, back, renewed_block, s3, r3)
         out = pltpu.make_async_copy(
             fresh[i], new_out.at[:, pl.ds(i * H, H)], out_sem.at[i]
         )
         out.start()
         out_copies.append(out)
 
-    for i in range(PIECES):
-        all_slots(back.at[i], fetched[i], s3.at[i], r3.at[i]).wait_recv()
+    for u, (i, lo, hi) in enumerate(units):
+        unit_done(u, back, s3, r3).wait_recv()
         for s in range(N_CTR):
             for j in range(CANDS):
-                stat[j * H : (j + 1) * H, :] = fetched[i][ours_at[s, 2, j]]
-
+                stat[j * H : (j + 1) * H, lo:hi] = fetched[u][ours_at[s, 2, j]]
             similar = lax.dot_general(
-                stat[0 : CANDS * H, :], rows[s * RB : (s + 1) * RB, :], (((1,), (1,)), ((), ())),
+                stat[0:G, lo:hi], rows[s * RB : (s + 1) * RB, lo:hi], (((1,), (1,)), ((), ())),
                 preferred_element_type=jnp.float32,
             )
+            if lo == 0 and hi < D:
+                ex[s, 0] = similar
+                continue
+            if lo > 0:
+                similar = similar + ex[s, 0]
             best = jnp.max(similar, axis=0, keepdims=True)
             if i > 0:
                 best = jnp.maximum(best, bb[s, 0:1, :])
@@ -450,9 +489,10 @@
     for copy in best_sends:
         copy.start()
     for i in range(PIECES):
-        all_slots(stage.at[i], landed[i], s2.at[i], r2.at[i]).wait_send()
-        all_slots(back.at[i], fetched[i], s3.at[i], r3.at[i]).wait_send()
+        sums_done(i).wait_send()
         out_copies[i].wait()
+    for u in range(len(units)):
+        unit_done(u, back, s3, r3).wait_send()
     for copy in best_sends:
         copy.wait()
     best = bb[0, 0:1, :]
@@ -482,6 +522,7 @@
     held = width // PIECES
     bf16, f32 = jnp.bfloat16, jnp.float32
     piece = pltpu.VMEM((N_ROW, held, features), bf16)
+    half_piece = pltpu.VMEM((N_ROW, held, features // 2), bf16)
     dma = pltpu.SemaphoreType.DMA
     renewed, nearest = pl.pallas_call(
         kernel,
@@ -500,7 +541,9 @@
             pltpu.VMEM((blocks, width, features), bf16),
             pltpu.VMEM((PIECES, N_ROW, held, features), bf16),
             pltpu.VMEM((PIECES, N_ROW, held, features), bf16),
-            *([piece] * 8),
+            *([piece] * 3),
+            *([half_piece] * 2),
+            *([piece] * 4),
             pltpu.VMEM((N_CTR, PIECES, CANDS * held, rb), f32),
             pltpu.VMEM((4 * N_CTR, rb), f32),
             pltpu.VMEM((N_CTR, CANDS + 1, held, rb), bf16),
@@ -524,7 +567,7 @@
             dma((1,)),
             dma((18,)),
             dma((18,)),
-            *([dma((PIECES,))] * 6),
+            *([dma((PIECES + 1,))] * 6),
             *([dma((N_CTR,))] * 4),
             dma((PIECES,)),
         ],

time: 252 us -> 248 us (0.984)
  Pallas kernels: 251 us -> 247 us
    pallas_call x1, Pallas kernels: 247 us -> 244 us  [on_device(): pl.pallas_call(kernel, out_shape=(jax.ShapeDtypeStruct(centroids.shape, b...]
where the time goes in v5:
time: 248 us
  Pallas kernels  247 us (100%)
    pallas_call x1, Pallas kernels, on_device(): pl.pallas_call(kernel, out_shape=(jax.ShapeDtypeStruct(centroids.shape, b...  244 us

profile of v5, /device:TPU:0, one launch (start us, length us, event | category | flops | bytes accessed | tf_op | source)
XLA Modules:
  0.0 247.9 jit_solution(9623576060220928951)
XLA Ops:
  0.6 243.9 %shard_map.50 = (bf16[16,64,1536]{2,1,0:T(8,128)(2,1)}, f32[768]{0:T(1024)}) custom-call(s32[1,6]{1,0:T(1,128)} %lists.1, bf16[768,1536]{1,0:T(8,128)(2,1)} %emb_in.1, bf16[16,64,1536]{2,1,0:T(8,128)(2,1)} %cent_in.1), custom_call_target="tpu_custom_call" | custom-call | tf_op jit(solution)/shard_map/pallas_call | solution.py:527
  244.6 3.2 %shard_map.51 = (bf16[16,64,1536]{2,1,0:T(8,128)(2,1)}, f32[768]{0:T(1024)}) custom-call(bf16[16,64,1536]{2,1,0:T(8,128)(2,1)} %get-tuple-element.4.renewed, f32[768]{0:T(1024)} %get-tuple-element.5.nearest), custom_call_target="tpu_custom_call" | custom-call | tf_op jit(solution)/shard_map/pallas_call | solution.py:578

commit v6 on v5

--- a/solution.py
+++ b/solution.py
@@ -30,14 +30,14 @@
 
 
 def steps(t):
-    return lax.rem(t * 5, N_ROW)
+    return lax.rem(t * 27, N_ROW)
 
 
 def slot_from(owner, row):
     dz = (row // 8 - owner // 8 + 4) % 4
     dy = ((row // 2) % 4 - (owner // 2) % 4 + 4) % 4
     dc = (row % 2 - owner % 2 + 2) % 2
-    return (dz * 8 + dy * 2 + dc) * 13 % N_ROW
+    return (dz * 8 + dy * 2 + dc) * 19 % N_ROW
 
 
 def kernel(
@@ -194,11 +194,11 @@
     asks[0] = mine[...]
 
     for t in range(1, N_ROW):
-        k = t * 5 % N_ROW
+        k = t * 27 % N_ROW
         back_k = (4 - k // 8) % 4 * 8 + (4 - (k // 2) % 4) % 4 * 2 + k % 2
         pltpu.make_async_remote_copy(
-            src_ref=mine,
-            dst_ref=asks.at[t],
+            src_ref=mine.at[pl.ds(0, 1)],
+            dst_ref=asks.at[t, pl.ds(0, 1)],
             send_sem=gs.at[0],
             recv_sem=gr.at[0],
             device_id=(ahead(back_k), ctr),
@@ -211,8 +211,8 @@
         to_left[PARTS - 1 - p].start()
 
     asked = pltpu.make_async_remote_copy(
-        src_ref=asks.at[pl.ds(1, N_ROW - 1)],
-        dst_ref=asks.at[pl.ds(1, N_ROW - 1)],
+        src_ref=asks.at[pl.ds(1, N_ROW - 1), pl.ds(0, 1)],
+        dst_ref=asks.at[pl.ds(1, N_ROW - 1), pl.ds(0, 1)],
         send_sem=gs.at[0],
         recv_sem=gr.at[0],
         device_id=(row, ctr),

time: 248 us -> 246 us (level)
  no operation moved by 1% of the time
where the time goes in v6:
time: 246 us
  Pallas kernels  245 us (100%)
    pallas_call x1, Pallas kernels, on_device(): pl.pallas_call(kernel, out_shape=(jax.ShapeDtypeStruct(centroids.shape, b...  242 us

profile of v6, /device:TPU:0, one launch (start us, length us, event | category | flops | bytes accessed | tf_op | source)
XLA Modules:
  0.0 245.7 jit_solution(10359040984859816691)
XLA Ops:
  0.6 241.7 %shard_map.50 = (bf16[16,64,1536]{2,1,0:T(8,128)(2,1)}, f32[768]{0:T(1024)}) custom-call(s32[1,6]{1,0:T(1,128)} %lists.1, bf16[768,1536]{1,0:T(8,128)(2,1)} %emb_in.1, bf16[16,64,1536]{2,1,0:T(8,128)(2,1)} %cent_in.1), custom_call_target="tpu_custom_call" | custom-call | tf_op jit(solution)/shard_map/pallas_call | solution.py:527
  242.4 3.2 %shard_map.51 = (bf16[16,64,1536]{2,1,0:T(8,128)(2,1)}, f32[768]{0:T(1024)}) custom-call(bf16[16,64,1536]{2,1,0:T(8,128)(2,1)} %get-tuple-element.4.renewed, f32[768]{0:T(1024)} %get-tuple-element.5.nearest), custom_call_target="tpu_custom_call" | custom-call | tf_op jit(solution)/shard_map/pallas_call | solution.py:578

commit v7 on v6

--- a/solution.py
+++ b/solution.py
@@ -30,14 +30,14 @@
 
 
 def steps(t):
-    return lax.rem(t * 27, N_ROW)
+    return lax.rem(t * 23, N_ROW)
 
 
 def slot_from(owner, row):
     dz = (row // 8 - owner // 8 + 4) % 4
     dy = ((row // 2) % 4 - (owner // 2) % 4 + 4) % 4
     dc = (row % 2 - owner % 2 + 2) % 2
-    return (dz * 8 + dy * 2 + dc) * 19 % N_ROW
+    return (dz * 8 + dy * 2 + dc) * 7 % N_ROW
 
 
 def kernel(
@@ -194,7 +194,7 @@
     asks[0] = mine[...]
 
     for t in range(1, N_ROW):
-        k = t * 27 % N_ROW
+        k = t * 23 % N_ROW
         back_k = (4 - k // 8) % 4 * 8 + (4 - (k // 2) % 4) % 4 * 2 + k % 2
         pltpu.make_async_remote_copy(
             src_ref=mine.at[pl.ds(0, 1)],
@@ -502,16 +502,17 @@
 
 
 def hand_over(renewed, nearest, new_out, near_out, hold, near_hold, sems, outs):
-    blocks = renewed.shape[0]
-    ins = [pltpu.make_async_copy(renewed.at[b], hold.at[b], sems.at[b]) for b in range(blocks)]
+    blocks = renewed.shape[0] // 2
+    two = [pl.ds(2 * b, 2) for b in range(blocks)]
+    ins = [pltpu.make_async_copy(renewed.at[p], hold.at[p], sems.at[b]) for b, p in enumerate(two)]
     ins.append(pltpu.make_async_copy(nearest, near_hold, sems.at[blocks]))
-    away = [pltpu.make_async_copy(hold.at[b], new_out.at[b], outs.at[b]) for b in range(blocks)]
+    away = [pltpu.make_async_copy(hold.at[p], new_out.at[p], outs.at[b]) for b, p in enumerate(two)]
     away.append(pltpu.make_async_copy(near_hold, near_out, outs.at[blocks]))
     for copy in ins:
         copy.start()
-    for one, two in zip(ins, away):
-        one.wait()
-        two.start()
+    for inward, outward in zip(ins, away):
+        inward.wait()
+        outward.start()
     for copy in away:
         copy.wait()
 

time: 246 us -> 247 us (level)
  no operation moved by 1% of the time
where the time goes in v7:
time: 247 us
  Pallas kernels  246 us (100%)
    pallas_call x1, Pallas kernels, on_device(): pl.pallas_call(kernel, out_shape=(jax.ShapeDtypeStruct(centroids.shape, b...  244 us

profile of v7, /device:TPU:0, one launch (start us, length us, event | category | flops | bytes accessed | tf_op | source)
XLA Modules:
  0.0 247.3 jit_solution(16294303471310532900)
XLA Ops:
  0.6 243.5 %shard_map.50 = (bf16[16,64,1536]{2,1,0:T(8,128)(2,1)}, f32[768]{0:T(1024)}) custom-call(s32[1,6]{1,0:T(1,128)} %lists.1, bf16[768,1536]{1,0:T(8,128)(2,1)} %emb_in.1, bf16[16,64,1536]{2,1,0:T(8,128)(2,1)} %cent_in.1), custom_call_target="tpu_custom_call" | custom-call | tf_op jit(solution)/shard_map/pallas_call | solution.py:528
  244.2 2.9 %shard_map.51 = (bf16[16,64,1536]{2,1,0:T(8,128)(2,1)}, f32[768]{0:T(1024)}) custom-call(bf16[16,64,1536]{2,1,0:T(8,128)(2,1)} %get-tuple-element.4.renewed, f32[768]{0:T(1024)} %get-tuple-element.5.nearest), custom_call_target="tpu_custom_call" | custom-call | tf_op jit(solution)/shard_map/pallas_call | solution.py:579
